TPU v7x, 256 devices: a whole 4x4x8 slice. The times are simulated.
256 devices in a mesh: expert: 4 (over x), tensor: 32 (over y, z_lo, core), dp: 2 (over z_hi).
Axes of the slice: x: 4, y: 4, z: 8 (z_hi: 2, z_lo: 4; z = z_hi * 4 + z_lo), core: 2. Of those that a mesh axis runs over, the one named last changes fastest.
Arguments:
- tokens: bfloat16 [2048, 6144], P(('expert', 'dp'), 'tensor'), may hold values from -250 to 250
- norm_gain: bfloat16 [6144], P('tensor'), may hold values from 0.25 to 1.75
- expert_ids: int32 [2048, 2], P(('expert', 'dp')), may hold values from 0 to 7, as said below
- route_weights: float32 [2048, 2], P(('expert', 'dp')), may hold values from 0.1 to 1
- gate_weight: bfloat16 [8, 6144, 11264], P(('expert', 'dp'), None, 'tensor'), may hold values from -0.078125 to 0.078125
- up_weight: bfloat16 [8, 6144, 11264], P(('expert', 'dp'), None, 'tensor'), may hold values from -0.078125 to 0.078125
- down_weight: bfloat16 [8, 11264, 6144], P(('expert', 'dp'), 'tensor'), may hold values from -0.0546875 to 0.0546875
Outputs:
- moe_out: bfloat16 [2048, 6144], P(('expert', 'dp'), 'tensor')
Inputs may be any that keep to these rules, and one draw needn't show every extreme that they name: `expert_ids`: each row names two different experts. Within each group of 256 consecutive rows no expert is named by more than 128 rows, and one and the same expert is named by exactly 128 rows in every group.
All inputs are finite; a program needn't handle non-finite values.
Results may differ from a plain program's by a relative error of at most 0.034.
Values may be sent and summed in bfloat16 or wider, within the bound.
A program may use at most 128 MiB of HBM per device.

v0:
```python
import jax
import jax.numpy as jnp
from jax import lax
from jax.sharding import PartitionSpec as P

D = 6144


norm_eps = 1e-05


def slot_targets(group_ids, capacity, expert_count):
    labels = jnp.arange(expert_count, dtype=jnp.int32)[None, :]
    first_hits = (group_ids[:, 0:1] == labels).astype(jnp.int32)
    second_hits = (group_ids[:, 1:2] == labels).astype(jnp.int32)
    both_hits = first_hits + second_hits
    earlier = jnp.cumsum(both_hits, axis=0) - both_hits
    first_slot = jnp.sum(earlier * first_hits, axis=1)
    second_slot = jnp.sum(earlier * second_hits, axis=1)
    first_dest = group_ids[:, 0] * capacity + first_slot
    second_dest = group_ids[:, 1] * capacity + second_slot
    return (first_dest, second_dest)


def per_device(tokens, norm_gain, expert_ids, route_weights, gate_weight, up_weight, down_weight):
    tok_rows = tokens.shape[0]
    width_share = tokens.shape[1]
    capacity = tok_rows // 2
    expert_count = lax.axis_size("expert") * lax.axis_size("dp")
    first_dest, second_dest = slot_targets(expert_ids, capacity, expert_count)
    places = jnp.arange(expert_count * capacity, dtype=jnp.int32)
    select = (
        (places[:, None] == first_dest[None, :]) | (places[:, None] == second_dest[None, :])
    ).astype(jnp.bfloat16)
    gate_cols = gate_weight[0]
    up_cols = up_weight[0]
    down_rows = down_weight[0]
    widened = tokens.astype(jnp.float32)
    squares = lax.psum(jnp.sum(widened * widened, axis=1, keepdims=True), "tensor")
    normed = (
        widened * lax.rsqrt(squares / D + norm_eps) * norm_gain.astype(jnp.float32)[None, :]
    ).astype(jnp.bfloat16)
    outgoing = jnp.dot(select, normed, preferred_element_type=jnp.float32).astype(jnp.bfloat16)
    outgoing = outgoing.reshape(expert_count, capacity, width_share)
    arrived = lax.all_to_all(outgoing, ("expert", "dp"), split_axis=0, concat_axis=0, tiled=True)
    column_block = lax.all_gather(arrived, "tensor", axis=2, tiled=True)
    block_width = column_block.shape[2]
    block_rows = column_block.reshape(-1, block_width)
    gate_val = jnp.dot(block_rows, gate_cols, preferred_element_type=jnp.float32)
    up_val = jnp.dot(block_rows, up_cols, preferred_element_type=jnp.float32)
    hidden = (jax.nn.silu(gate_val) * up_val).astype(jnp.bfloat16)
    summed = lax.psum_scatter(
        lax.dot_general(
            down_rows, hidden, (((0,), (1,)), ((), ())), preferred_element_type=jnp.float32
        ).astype(jnp.bfloat16),
        "tensor",
        scatter_dimension=0,
        tiled=True,
    )
    shaped = summed.reshape(width_share, expert_count, capacity)
    returned = lax.all_to_all(shaped, ("expert", "dp"), split_axis=1, concat_axis=1, tiled=True)
    returned = returned.reshape(width_share, expert_count * capacity)
    targets = jnp.concatenate([first_dest, second_dest], axis=0)
    pick_table = (targets[:, None] == places[None, :]).astype(jnp.bfloat16)
    picked = lax.dot_general(
        pick_table, returned, (((1,), (1,)), ((), ())), preferred_element_type=jnp.float32
    )
    combined = route_weights[:, 0:1] * picked[:tok_rows] + route_weights[:, 1:2] * picked[tok_rows:]
    return combined.astype(jnp.bfloat16)


def solution(mesh):
    placed = (
        P(("expert", "dp"), "tensor"),
        P("tensor"),
        P(("expert", "dp"), None),
        P(("expert", "dp"), None),
        P(("expert", "dp"), None, "tensor"),
        P(("expert", "dp"), None, "tensor"),
        P(("expert", "dp"), "tensor", None),
    )
    return jax.shard_map(
        per_device,
        mesh=mesh,
        in_specs=placed,
        out_specs=P(("expert", "dp"), "tensor"),
        check_vma=False,
    )
```

profile of v0, /device:TPU:1, one launch (start us, length us, event | category | flops | bytes accessed | tf_op | source)
XLA Modules:
  0.0 421.9 jit_solution(267769398834274216)
XLA Ops:
  6.5 0.0 all-gather.2.cloned.1.call-start
  6.5 0.8 fusion.37
  7.3 0.6 reduce-window.6
  7.9 0.2 slice_reduce_fusion
  8.1 0.9 fusion.28
  9.1 70.0 %psum.7 = f32[256,1]{0,1:T(1,128)S(1)} all-reduce(f32[256,1]{0,1:T(1,128)S(1)} %bitcast.66), channel_id=1, replica_groups=mesh['expert'=4,'tensor'=32,'dp'=2] {'tensor'}, use_global_device_ids=true, to_apply=%region_5.6 | all-reduce | flops 256 | bytes 2048 | tf_op jit(solution)/shard_map/psum | solution.py:39
  79.1 0.7 convert_element_type.45
  79.8 0.1 select_reduce_fusion.1
  79.9 1.3 fusion.20
  81.2 0.1 copy.37
  81.3 19.6 %all_to_all.10 = bf16[8,128,192]{1,2,0:T(8,128)(2,1)S(1)} all-to-all(bf16[8,128,192]{1,2,0:T(8,128)(2,1)S(1)} %bitcast.59), channel_id=1, replica_groups=mesh['expert'=4,'tensor'=32,'dp'=2] {'expert','dp'}, dimensions={0} | all-to-all | bytes 786432 | tf_op jit(solution)/shard_map/all_to_all | solution.py:45
  100.9 0.0 slice-start
  100.9 1.0 copy.12
  101.9 0.0 all-gather.2.cloned.1.call-update
  101.9 0.0 reduce-scatter.4.cloned.1.call-start
  102.0 77.0 %all-gather.2.cloned.1.call-done = bf16[8,128,6144]{1,0,2:T(8,128)(2,1)} async-done(((bf16[8,128,192]{1,0,2:T(8,128)(2,1)}), bf16[8,128,6144]{1,0,2:T(8,128)(2,1)}) %all-gather.2.cloned.1.call-update) | async-done | bytes 12582928 | tf_op jit(solution)/shard_map/all_gather | solution.py:46
  178.9 10.6 %fusion = f32[1024,352]{0,1:T(8,128)S(1)} fusion(bf16[768,8,8,128]{3,2,1,0:T(8,128)(2,1)} %bitcast.70, bf16[1,6144,352]{1,2,0:T(8,128)(2,1)} %param.11), kind=kOutput, calls=%fused_computation | convolution fusion | flops 4429185024 | bytes 18350080 | tf_op jit(solution)/shard_map/dot_general | solution.py:49
  189.6 0.0 slice-done
  189.6 0.0 copy-done.1
  189.6 0.0 slice-done.1
  189.6 4.7 %fusion.15 = bf16[1024,352]{0,1:T(8,128)(2,1)S(1)} fusion(bf16[768,8,8,128]{3,2,1,0:T(8,128)(2,1)S(1)} %bitcast.71, bf16[1,6144,352]{1,2,0:T(8,128)(2,1)S(1)} %bitcast.73, f32[1024,352]{0,1:T(8,128)S(1)} %fusion), kind=kOutput, calls=%fused_computation.13 | convolution fusion | flops 4431347712 | bytes 19070976 | tf_op jit(solution)/shard_map/dot_general | solution.py:50
  194.4 11.8 %convert_bitcast_fusion = bf16[6144,1024]{0,1:T(8,128)(2,1)} fusion(bf16[1024,352]{0,1:T(8,128)(2,1)S(1)} %fusion.15, bf16[1,352,6144]{2,1,0:T(8,128)(2,1)} %param.13), kind=kOutput, calls=%fused_computation.4 | convolution fusion | flops 4435476480 | bytes 17629184 | tf_op jit(solution)/shard_map/dot_general | solution.py:53
  206.2 16.6 %copy.15 = bf16[6144,1024]{1,0:T(8,128)(2,1)} copy(bf16[6144,1024]{0,1:T(8,128)(2,1)} %convert_bitcast_fusion) | data formatting | bytes 25165824
  222.8 0.0 reduce-scatter.4.cloned.1.call-update
  222.8 170.2 %reduce-scatter.4.cloned.1.call-done = bf16[192,1024]{1,0:T(8,128)(2,1)} async-done(((bf16[6144,1024]{1,0:T(8,128)(2,1)}), bf16[192,1024]{1,0:T(8,128)(2,1)}) %reduce-scatter.4.cloned.1.call-update) | async-done | bytes 393232
  393.0 1.2 copy.16
  394.2 0.9 copy.13
  395.1 7.9 %all-to-all-start.1 = ((bf16[192,8,128]{2,0,1:T(8,128)(2,1)}), bf16[192,8,128]{2,0,1:T(8,128)(2,1)S(1)}, u32[]{:S(2)}, u32[]{:S(2)}) async-start(bf16[192,8,128]{2,0,1:T(8,128)(2,1)} %copy.13), calls=%async_computation.1 | async-start | bytes 786432 | tf_op jit(solution)/shard_map/all_to_all | solution.py:61
  403.0 0.0 copy-done
  403.0 10.7 %all-to-all-done.1 = bf16[192,8,128]{2,0,1:T(8,128)(2,1)S(1)} async-done(((bf16[192,8,128]{2,0,1:T(8,128)(2,1)}), bf16[192,8,128]{2,0,1:T(8,128)(2,1)S(1)}, u32[]{:S(2)}, u32[]{:S(2)}) %all-to-all-start.1) | async-done | bytes 393248 | tf_op jit(solution)/shard_map/all_to_all | solution.py:61
  413.8 0.7 fusion.9
  414.4 0.7 fusion.32
  (11 shorter events, 0.1 us)
Async XLA Ops:
  6.5 172.4 %all-gather.2.cloned.1.call-start = ((), (), s32[]{:S(2)}) async-start(), calls=%async_computation.3 | async-start | bytes 12976128 | tf_op jit(solution)/shard_map/all_gather | solution.py:46
  100.9 88.7 %slice-start = ((s8[4325376]{0:T(1024)(128)(4,1)}), s8[131072]{0:T(1024)(128)(4,1)S(1)}, s32[]{:S(2)}) async-start(s8[4325376]{0:T(1024)(128)(4,1)} %bitcast.72), calls=%async_computation.5 | async-start | bytes 262144
  101.9 291.1 %reduce-scatter.4.cloned.1.call-start = ((), (), s32[]{:S(2)}) async-start(), calls=%async_computation.4 | async-start | bytes 12976128
  178.9 10.7 %copy-start.1 = (bf16[8,128,6144]{1,0,2:T(8,128)(2,1)S(1)}, bf16[8,128,6144]{1,0,2:T(8,128)(2,1)}, u32[]{:S(2)}) copy-start(bf16[8,128,6144]{1,0,2:T(8,128)(2,1)} %all-gather.2.cloned.1.call-done) | copy-start | bytes 37748740
  178.9 10.7 %slice-start.1 = ((s8[4325376]{0:T(1024)(128)(4,1)}), s8[4194304]{0:T(1024)(128)(4,1)S(1)}, s32[]{:S(2)}) async-start(s8[4325376]{0:T(1024)(128)(4,1)} %bitcast.72), calls=%async_computation.6 | async-start | bytes 8388608
  222.8 180.2 %copy-start = (f32[256,2]{0,1:T(2,128)S(1)}, f32[256,2]{0,1:T(2,128)}, u32[]{:S(2)}) copy-start(f32[256,2]{0,1:T(2,128)} %param.10) | copy-start | bytes 6148
  395.1 18.6 %all-to-all-start.1 = ((bf16[192,8,128]{2,0,1:T(8,128)(2,1)}), bf16[192,8,128]{2,0,1:T(8,128)(2,1)S(1)}, u32[]{:S(2)}, u32[]{:S(2)}) async-start(bf16[192,8,128]{2,0,1:T(8,128)(2,1)} %copy.13), calls=%async_computation.1 | async-start | bytes 786432 | tf_op jit(solution)/shard_map/all_to_all | solution.py:61
Sparse Core Ops, SparseCore 0:
  102.1 76.8 all-gather.1
  223.0 169.9 reduce-scatter.3
where the time goes:
time: 425 us; the launch traced here: 422 us
  waiting for transfers between devices  258 us (61%)
  blocking collectives  89.6 us (21%)
  matrix products  29.2 us (7%)
  local copies, waits for them, and re-layouts  20.9 us (5%)
  between operations  13.5 us (3%)
  starting transfers between devices  7.92 us (2%)
    unnamed x3, waiting for transfers between devices  170 us
    all_gather x1, waiting for transfers between devices, per_device(): column_block = lax.all_gather(arrived, 'tensor', axis=2, tiled=True)  77 us
    psum x1, blocking collectives, per_device(): lax.psum(jnp.sum(widened * widened, axis=1, keepdims=True), 'tensor')  70 us
    all_to_all x1, blocking collectives, per_device(): lax.all_to_all(outgoing, ('expert', 'dp'), split_axis=0, concat_axis=0, t...  19.6 us
    unnamed x10, local copies, waits for them, and re-layouts  17.8 us
    dot_general x1, matrix products, per_device(): lax.dot_general(down_rows, hidden, (((0,), (1,)), ((), ())), preferred_el...  11.8 us
    all_to_all x1, waiting for transfers between devices, per_device(): lax.all_to_all(shaped, ('expert', 'dp'), split_axis=1, concat_axis=1, til...  10.7 us
    dot_general x1, matrix products, per_device(): jnp.dot(block_rows, gate_cols, preferred_element_type=jnp.float32)  10.6 us
  transfers between devices with their start and end apart: 3, of which 3 were waited for; matrix products, arithmetic and copies ran while one was open for 0% of the time, Pallas kernels for 0%

commit v1 on v0

v1 whole, which is shorter than its diff:
```python
import jax
import jax.numpy as jnp
from jax import lax
from jax.experimental import pallas as pl
from jax.experimental.pallas import tpu as pltpu
from jax.sharding import PartitionSpec as P

D = 6144
NORM_EPS = 1e-05
MESH = pl.DeviceIdType.MESH
NX, NY, NZ, ND = 4, 4, 4, 2
GROUP = 256
CAP = 128
HALF = CAP // 2
FEAT = 384
HID = 352
ROUTES = ((0, 0), (1, 0), (0, 1), (1, 1), (2, 1), (3, 1), (2, 0), (3, 0))
PER = 2
CHUNKS = len(ROUTES) // PER
ROWS = PER * HALF
STEPS = CHUNKS * NZ
SECOND, THIRD, MULTIPLY = 2, 4, 5
FARTHEST, NEIGHBOURS, FINISH = 1, 3, 5
LAG = NZ + MULTIPLY
F32 = jnp.float32
BF16 = jnp.bfloat16


def xor4(a, b):
    low = lax.rem(lax.rem(a, 2) + lax.rem(b, 2), 2)
    high = lax.rem(lax.div(a, 2) + lax.div(b, 2), 2)
    return low + 2 * high


def kernel(
    tok_hbm, gain_ref, ids_hbm, rw_hbm, wg_hbm, wu_hbm, wd_hbm,
    out_ref,
    wgu, wd, x, scaled, acc, sq, hid, gains,
    ids_ref, rw_ref, tokx, sibtok, stage, mine, given, srecv, halves, fulls, zrecv, ret, part, partr,
    wsem, dsem, tok_s, tok_r, disp_s, disp_r, gz_s, gz_r, gy_s, gy_r, gf_s, gf_r,
    z_s, z_r, y_s, y_r, f_s, f_r, b_s, b_r,
    sib_s, sib_r, h_s, h_r, w_s, w_r, zz_s, zz_r, ret_s, ret_r, part_s, part_r,
):
    xi = lax.axis_index("expert")
    di = lax.axis_index("dp")
    me = lax.axis_index("tensor")
    c = lax.rem(me, 2)
    z = lax.rem(lax.div(me, 2), NZ)
    y = lax.div(me, 2 * NZ)
    own = y * NZ + z
    yp = lax.rem(y + 1, NY)
    ym = lax.rem(y + NY - 1, NY)

    def tid(yy, zz, cc):
        return (yy * NZ + zz) * 2 + cc

    sib = {"tensor": tid(y, z, 1 - c)}
    up = {"tensor": tid(yp, z, c)}
    down = {"tensor": tid(ym, z, c)}

    def zdev(i):
        return {"tensor": tid(y, xor4(z, i), c)}

    def expert_of(k):
        dx, dd = ROUTES[k]
        return {"expert": lax.rem(xi + dx, NX), "dp": lax.rem(di + dd, ND)}

    def group_of(k):
        dx, dd = ROUTES[k]
        return {"expert": lax.rem(xi + NX - dx, NX), "dp": lax.rem(di + dd, ND)}

    def rcopy(src, dst, ssem, rsem, dev):
        return pltpu.make_async_remote_copy(
            src_ref=src, dst_ref=dst, send_sem=ssem, recv_sem=rsem, device_id=dev, device_id_type=MESH
        )

    barrier = pltpu.get_barrier_semaphore()
    partners = [sib, up, down] + [zdev(i) for i in range(1, NZ)] + [expert_of(k) for k in range(1, len(ROUTES))]
    for dev in partners:
        pl.semaphore_signal(barrier, inc=1, device_id=dev, device_id_type=MESH)

    share = FEAT // 2
    small = [
        pltpu.make_async_copy(ids_hbm, ids_ref, wsem.at[0]),
        pltpu.make_async_copy(tok_hbm, tokx.at[pl.ds(0, share)], wsem.at[1]),
        pltpu.make_async_copy(rw_hbm, rw_ref, wsem.at[2]),
    ]
    for load in small:
        load.start()
    tokx[share:, :] = jnp.zeros((16, GROUP), BF16)
    tokx[share:, 0:share] = jnp.broadcast_to(gain_ref[...].astype(F32).reshape(1, share), (16, share)).astype(BF16)

    before = (
        lax.broadcasted_iota(jnp.int32, (GROUP, GROUP), 0) < lax.broadcasted_iota(jnp.int32, (GROUP, GROUP), 1)
    ).astype(F32).astype(BF16)
    labels = lax.broadcasted_iota(jnp.int32, (16, GROUP), 0)
    spot = lax.broadcasted_iota(jnp.int32, (HALF, 1), 0) + HALF * c
    place = []
    for k in range(len(ROUTES)):
        dev = expert_of(k)
        place.append(spot + (dev["expert"] * ND + dev["dp"]) * CAP)
    place = jnp.concatenate(place, axis=0)
    small[0].wait()
    e0 = ids_ref[0:1, :]
    e1 = ids_ref[1:2, :]
    hit0 = (e0 == labels).astype(F32)
    hit1 = (e1 == labels).astype(F32)
    earlier = jnp.dot((hit0 + hit1).astype(BF16), before, preferred_element_type=F32)
    slot0 = jnp.sum(earlier * hit0, axis=0, keepdims=True).astype(jnp.int32)
    slot1 = jnp.sum(earlier * hit1, axis=0, keepdims=True).astype(jnp.int32)
    dest0 = e0 * CAP + slot0
    dest1 = e1 * CAP + slot1
    small[1].wait()

    pl.semaphore_wait(barrier, len(partners))

    tok_copy = rcopy(tokx, sibtok, tok_s, tok_r, sib)
    tok_copy.start()
    select = ((place == dest0) | (place == dest1)).astype(F32).astype(BF16)

    loads = []
    for zz in range(NZ):
        for yy in range(NY):
            for k, source in enumerate((wg_hbm, wu_hbm)):
                loads.append(
                    pltpu.make_async_copy(
                        source.at[0, :, pl.ds((yy * NZ + zz) * FEAT, FEAT)],
                        wgu.at[zz, pl.ds(k * HID, HID), pl.ds(yy * FEAT, FEAT)],
                        wsem.at[3 + len(loads)],
                    )
                )
    dloads = [
        pltpu.make_async_copy(wd_hbm.at[0, :, pl.ds(j * FEAT, FEAT)], wd.at[j], dsem.at[j])
        for j in range(NY * NZ)
    ]

    tok_copy.wait_recv()
    here = tokx[...].astype(F32)
    there = sibtok[...].astype(F32)
    first_core = jnp.where(c == 0, here, there)
    second_core = jnp.where(c == 0, there, here)
    both = jnp.concatenate([first_core[:share], second_core[:share]], axis=0).astype(BF16)
    rows = lax.dot_general(
        select, both, (((1,), (1,)), ((), ())), preferred_element_type=F32
    ).astype(BF16)
    x[0, own, c, 0:HALF, :] = rows[0:HALF]

    def disp_copy(k):
        target = x.at[k // PER, own, c, pl.ds((k % PER) * HALF, HALF)]
        return rcopy(stage.at[k], target, disp_s.at[k], disp_r.at[k], expert_of(k))

    for k in range(1, len(ROUTES)):
        stage[k] = rows[k * HALF : (k + 1) * HALF]
        disp_copy(k).start()

    gain_row = jnp.concatenate(
        [first_core[share : share + 1, 0:share], second_core[share : share + 1, 0:share]], axis=1
    )
    index = lax.broadcasted_iota(jnp.int32, (16, 128), 0)
    tile = jnp.zeros((16, 128), F32)
    for j in range(3):
        tile = jnp.where(index == j, jnp.broadcast_to(gain_row[:, 128 * j : 128 * (j + 1)], (16, 128)), tile)
    gains[y, z] = tile.astype(BF16)

    def gzc(i):
        return rcopy(gains.at[y, z], gains.at[y, z], gz_s.at[i], gz_r.at[i], zdev(i))

    def gyc(i, way):
        ref = gains.at[y, xor4(z, i)]
        return rcopy(ref, ref, gy_s.at[i, way], gy_r.at[i, way], (up, down)[way])

    def gfc(i):
        ref = gains.at[ym, xor4(z, i)]
        return rcopy(ref, ref, gf_s.at[i], gf_r.at[i], up)

    for i in range(1, NZ):
        gzc(i).start()

    def at_step(s):
        q = lax.div(s, NZ)
        i = lax.rem(s, NZ)
        return q, i, xor4(z, i)

    def zc(q, i):
        return rcopy(x.at[q, own, c], x.at[q, own, c], z_s.at[q, i], z_r.at[q, i], zdev(i))

    def yc(s, way):
        q, i, zi = at_step(s)
        b = y * NZ + zi
        return rcopy(x.at[q, b, c], x.at[q, b, c], y_s.at[s, way], y_r.at[s, way], (up, down)[way])

    def fc(s, way):
        q, i, zi = at_step(s)
        b = (ym, yp)[way] * NZ + zi
        ref = x.at[q, b, c, pl.ds(way * (ROWS // 2), ROWS // 2)]
        return rcopy(ref, ref, f_s.at[s, way], f_r.at[s, way], (up, down)[way])

    def bc(s, r):
        q, i, zi = at_step(s)
        b = lax.rem(y + r, NY) * NZ + zi
        return rcopy(x.at[q, b, c], x.at[q, b, c], b_s.at[s, r], b_r.at[s, r], sib)

    def open_chunk(chunk):
        for k in range(max(1, chunk * PER), (chunk + 1) * PER):
            disp_copy(k).wait_recv()
        for j in range(1, NZ):
            zc(chunk, j).start()

    def first(s):
        q, i, zi = at_step(s)

        @pl.when(i > 0)
        def _():
            zc(q, i).wait_recv()

        yc(s, 0).start()
        yc(s, 1).start()
        bc(s, 0).start()

        @pl.when((s > 0) & (s < NZ))
        def _():
            gzc(i).wait_recv()

        @pl.when(s < NZ)
        def _():
            gyc(i, 0).start()
            gyc(i, 1).start()

        for chunk in range(1, CHUNKS):

            @pl.when(s == chunk * NZ - 1)
            def _():
                open_chunk(chunk)

    def second(s):
        q, i, zi = at_step(s)
        yc(s, 0).wait_recv()
        fc(s, 0).start()
        yc(s, 1).wait_recv()
        fc(s, 1).start()
        bc(s, 3).start()
        bc(s, 1).start()

        @pl.when(s < NZ)
        def _():
            gyc(i, 0).wait_recv()
            gfc(i).start()
            gyc(i, 1).wait_recv()

    def third(s):
        q, i, zi = at_step(s)
        fc(s, 0).wait_recv()
        fc(s, 1).wait_recv()
        bc(s, 2).start()

        @pl.when(s < NZ)
        def _():
            gfc(i).wait_recv()

    def gate_up(s):
        q, i, zi = at_step(s)
        for r in range(NY):
            bc(s, r).wait_recv()
        squares = sq[...]
        for yy in range(NY):
            block = x[q, yy * NZ + zi].reshape(2 * ROWS, FEAT)
            gain = gains[yy, zi].astype(F32)
            for j in range(3):
                slab = block[:, 128 * j : 128 * (j + 1)].astype(F32)
                squares = squares + slab * slab
                at = yy * FEAT + 128 * j
                scaled[:, at : at + 128] = (slab * gain[j : j + 1, :]).astype(BF16)
        sq[...] = squares
        acc[...] += lax.dot_general(
            scaled[...], wgu[zi], (((1,), (1,)), ((), ())), preferred_element_type=F32
        )

        @pl.when(i == NZ - 1)
        def _():
            total = jnp.sum(sq[...], axis=1, keepdims=True)
            scale = lax.rsqrt(total / D + NORM_EPS)
            gate = acc[:, 0:HID] * scale
            lift = acc[:, HID:] * scale
            value = (gate / (1.0 + jnp.exp(-gate)) * lift).astype(BF16)
            for h in range(2):
                hid[q, lax.rem(c + h, 2)] = value[h * ROWS : (h + 1) * ROWS]
            acc[...] = jnp.zeros_like(acc)
            sq[...] = jnp.zeros_like(sq)

    def out_step(s):
        return lax.div(s, NZ), (NZ - 1) - lax.rem(s, NZ)

    def sc(s, r):
        return rcopy(given.at[s, r], srecv.at[s, r], sib_s.at[s, r], sib_r.at[s, r], sib)

    def hc(s, way):
        span = pl.ds(way * (ROWS // 2), ROWS // 2)
        return rcopy(mine.at[s, 2, span], halves.at[s, way], h_s.at[s, way], h_r.at[s, way], (up, down)[way])

    def wc(s, way):
        return rcopy(mine.at[s, (1, 3)[way]], fulls.at[s, way], w_s.at[s, way], w_r.at[s, way], (up, down)[way])

    def zzc(s):
        q, i = out_step(s)
        return rcopy(mine.at[s, 0], zrecv.at[q, i], zz_s.at[q, i], zz_r.at[q, i], zdev(i))

    def retc(k):
        source = mine.at[k // PER * NZ + NZ - 1, 0, pl.ds((k % PER) * HALF, HALF)]
        return rcopy(source, ret.at[k], ret_s.at[k], ret_r.at[k], group_of(k))

    def produce(s):
        q, i = out_step(s)
        zi = xor4(z, i)
        left = hid[q].reshape(2 * ROWS, HID)
        for r in (2, 1, 3, 0):
            b = lax.rem(y + r, NY) * NZ + zi
            block = jnp.dot(left, wd[b], preferred_element_type=F32).astype(BF16)
            given[s, r] = block[ROWS:]
            sc(s, r).start()
            mine[s, r] = block[:ROWS]

    def chip_sum(s, r):
        sc(s, r).wait_recv()
        return mine[s, r].astype(F32) + srecv[s, r].astype(F32)

    def farthest(s):
        mine[s, 2] = chip_sum(s, 2).astype(BF16)
        hc(s, 0).start()
        hc(s, 1).start()

    def neighbours(s):
        half = ROWS // 2
        total = chip_sum(s, 1)
        hc(s, 0).wait_recv()
        total = jnp.concatenate([total[:half] + halves[s, 0].astype(F32), total[half:]], axis=0)
        mine[s, 1] = total.astype(BF16)
        wc(s, 0).start()
        total = chip_sum(s, 3)
        hc(s, 1).wait_recv()
        total = jnp.concatenate([total[:half], total[half:] + halves[s, 1].astype(F32)], axis=0)
        mine[s, 3] = total.astype(BF16)
        wc(s, 1).start()

    def finish(s):
        q, i = out_step(s)
        total = chip_sum(s, 0)
        wc(s, 0).wait_recv()
        total = total + fulls[s, 0].astype(F32)
        wc(s, 1).wait_recv()
        total = total + fulls[s, 1].astype(F32)

        @pl.when(i > 0)
        def _():
            mine[s, 0] = total.astype(BF16)
            zzc(s).start()

        @pl.when(i == 0)
        def _():
            whole = total
            for j in range(1, NZ):
                zzc(s - j).wait_recv()
                whole = whole + zrecv[q, j].astype(F32)
            whole = whole.astype(BF16)
            mine[s, 0] = whole

            @pl.when(q == 0)
            def _():
                ret[0] = whole[0:HALF]

            for chunk in range(CHUNKS):

                @pl.when(q == chunk)
                def _():
                    for k in range(max(1, chunk * PER), (chunk + 1) * PER):
                        retc(k).start()

    def step(t, carry):
        u = t - LAG
        stages = (
            (first, t, 0), (second, t, SECOND), (third, t, THIRD),
            (finish, u, FINISH), (neighbours, u, NEIGHBOURS), (farthest, u, FARTHEST),
            (gate_up, t, MULTIPLY), (produce, u, 0),
        )
        for stage_of, now, behind in stages:

            @pl.when((now >= behind) & (now < STEPS + behind))
            def _():
                stage_of(now - behind)

        return carry

    open_chunk(0)
    first(jnp.int32(0))
    for load in loads + dloads:
        load.start()
    acc[...] = jnp.zeros_like(acc)
    sq[...] = jnp.zeros_like(sq)
    for load in loads + dloads:
        load.wait()
    lax.fori_loop(1, LAG + STEPS + FINISH, step, 0)

    small[2].wait()
    combined = jnp.zeros((FEAT, GROUP), F32)
    for chunk in range(CHUNKS):
        for k in range(max(1, chunk * PER), (chunk + 1) * PER):
            retc(k).wait_recv()
        came = ret[chunk * PER : (chunk + 1) * PER].reshape(ROWS, FEAT)
        spots = place[chunk * ROWS : (chunk + 1) * ROWS]
        for k, dest in enumerate((dest0, dest1)):
            pick = (spots == dest).astype(F32).astype(BF16)
            combined += rw_ref[k : k + 1, :] * lax.dot_general(
                came, pick, (((0,), (0,)), ((), ())), preferred_element_type=F32
            )
    left = combined[:share]
    right = combined[share:]
    part[...] = jnp.where(c == 0, right, left)
    part_copy = rcopy(part, partr, part_s, part_r, sib)
    part_copy.start()
    kept = jnp.where(c == 0, left, right)
    part_copy.wait_recv()
    out_ref[...] = (kept + partr[...]).astype(BF16)

    part_copy.wait_send()
    tok_copy.wait_send()
    for k in range(1, len(ROUTES)):
        disp_copy(k).wait_send()
        retc(k).wait_send()
    for i in range(NZ):
        if i > 0:
            gzc(i).wait_send()
        gyc(i, 0).wait_send()
        gyc(i, 1).wait_send()
        gfc(i).wait_send()

    def drain(s, carry):
        for way in range(2):
            yc(s, way).wait_send()
            fc(s, way).wait_send()
            hc(s, way).wait_send()
            wc(s, way).wait_send()
        for r in range(NY):
            bc(s, r).wait_send()
            sc(s, r).wait_send()
        q, i, zi = at_step(s)

        @pl.when(i > 0)
        def _():
            zc(q, i).wait_send()

        q, i = out_step(s)

        @pl.when(i > 0)
        def _():
            zzc(s).wait_send()

        return carry

    lax.fori_loop(0, STEPS, drain, 0)


def per_device(tokens, norm_gain, expert_ids, route_weights, gate_weight, up_weight, down_weight):
    vmem = pl.BlockSpec(memory_space=pltpu.VMEM)
    hbm = pl.BlockSpec(memory_space=pl.ANY)
    blocks = NY * NZ
    dma = pltpu.SemaphoreType.DMA
    scratch = [
        pltpu.VMEM((NZ, 2 * HID, NY * FEAT), BF16),
        pltpu.VMEM((blocks, HID, FEAT), BF16),
        pltpu.VMEM((CHUNKS, blocks, 2, ROWS, FEAT), BF16),
        pltpu.VMEM((2 * ROWS, NY * FEAT), BF16),
        pltpu.VMEM((2 * ROWS, 2 * HID), F32),
        pltpu.VMEM((2 * ROWS, 128), F32),
        pltpu.VMEM((CHUNKS, 2, ROWS, HID), BF16),
        pltpu.VMEM((NY, NZ, 16, 128), BF16),
        pltpu.VMEM((2, GROUP), jnp.int32),
        pltpu.VMEM((2, GROUP), F32),
        pltpu.VMEM((FEAT // 2 + 16, GROUP), BF16),
        pltpu.VMEM((FEAT // 2 + 16, GROUP), BF16),
        pltpu.VMEM((len(ROUTES), HALF, FEAT), BF16),
        pltpu.VMEM((STEPS, NY, ROWS, FEAT), BF16),
        pltpu.VMEM((STEPS, NY, ROWS, FEAT), BF16),
        pltpu.VMEM((STEPS, NY, ROWS, FEAT), BF16),
        pltpu.VMEM((STEPS, 2, ROWS // 2, FEAT), BF16),
        pltpu.VMEM((STEPS, 2, ROWS, FEAT), BF16),
        pltpu.VMEM((CHUNKS, NZ, ROWS, FEAT), BF16),
        pltpu.VMEM((len(ROUTES), HALF, FEAT), BF16),
        pltpu.VMEM((FEAT // 2, GROUP), F32),
        pltpu.VMEM((FEAT // 2, GROUP), F32),
        dma((3 + 2 * blocks,)), dma((blocks,)),
        dma, dma, dma((len(ROUTES),)), dma((len(ROUTES),)),
        dma((NZ,)), dma((NZ,)), dma((NZ, 2)), dma((NZ, 2)), dma((NZ,)), dma((NZ,)),
        dma((CHUNKS, NZ)), dma((CHUNKS, NZ)), dma((STEPS, 2)), dma((STEPS, 2)),
        dma((STEPS, 2)), dma((STEPS, 2)), dma((STEPS, NY)), dma((STEPS, NY)),
        dma((STEPS, NY)), dma((STEPS, NY)), dma((STEPS, 2)), dma((STEPS, 2)),
        dma((STEPS, 2)), dma((STEPS, 2)), dma((CHUNKS, NZ)), dma((CHUNKS, NZ)),
        dma((len(ROUTES),)), dma((len(ROUTES),)), dma, dma,
    ]
    rows = CHUNKS * 2 * ROWS
    out = pl.pallas_call(
        kernel,
        out_shape=jax.ShapeDtypeStruct((FEAT // 2, GROUP), BF16),
        in_specs=[hbm, vmem, hbm, hbm, hbm, hbm, hbm],
        out_specs=vmem,
        scratch_shapes=scratch,
        cost_estimate=pl.CostEstimate(
            flops=6 * rows * D * HID, bytes_accessed=6 * D * HID, transcendentals=rows * HID
        ),
        compiler_params=pltpu.CompilerParams(
            collective_id=0, has_side_effects=True, vmem_limit_bytes=61 * 1024 * 1024
        ),
    )(
        tokens.T,
        norm_gain,
        expert_ids.T,
        route_weights.T,
        gate_weight.swapaxes(1, 2),
        up_weight.swapaxes(1, 2),
        down_weight,
    )
    return out.T


def solution(mesh):
    placed = (
        P(("expert", "dp"), "tensor"),
        P("tensor"),
        P(("expert", "dp"), None),
        P(("expert", "dp"), None),
        P(("expert", "dp"), None, "tensor"),
        P(("expert", "dp"), None, "tensor"),
        P(("expert", "dp"), "tensor", None),
    )
    return jax.shard_map(
        per_device,
        mesh=mesh,
        in_specs=placed,
        out_specs=P(("expert", "dp"), "tensor"),
        check_vma=False,
    )
```

time: 425 us -> 150 us (0.35)
  waiting for transfers between devices: 258 us -> 0 us
  Pallas kernels: 0 us -> 149 us
  blocking collectives: 89.6 us -> 0 us
  matrix products: 29.2 us -> 0 us
  local copies, waits for them, and re-layouts: 20.9 us -> 1.54 us
  between operations: 13.5 us -> 0.01 us
  starting transfers between devices: 7.92 us -> 0 us
    unnamed x3 -> x0, waiting for transfers between devices: 170 us -> none
    pallas_call x0 -> x1, Pallas kernels: none -> 149 us  [per_device(): pl.pallas_call(kernel, out_shape=jax.ShapeDtypeStruct((FEAT // 2, GROUP),...]
    all_gather x1 -> x0, waiting for transfers between devices: 77 us -> none  [per_device(): column_block = lax.all_gather(arrived, 'tensor', axis=2, tiled=True)]
    psum x1 -> x0, blocking collectives: 70 us -> none  [per_device(): lax.psum(jnp.sum(widened * widened, axis=1, keepdims=True), 'tensor')]
    dot_general x5 -> x0, matrix products: 29.2 us -> none  [the longest x1 11.8 us: per_device(): lax.dot_general(down_rows, hidden, (((0,), (1,)), ((), ())), preferred_el...]
    all_to_all x1 -> x0, blocking collectives: 19.6 us -> none  [per_device(): lax.all_to_all(outgoing, ('expert', 'dp'), split_axis=0, concat_axis=0, t...]
    unnamed x10 -> x1, local copies, waits for them, and re-layouts: 17.8 us -> 1.54 us
    all_to_all x1 -> x0, waiting for transfers between devices: 10.7 us -> none  [per_device(): lax.all_to_all(shaped, ('expert', 'dp'), split_axis=1, concat_axis=1, til...]
  transfers between devices with their start and end apart: 3 -> 0, of which waited for: 3 -> 0; matrix products, arithmetic and copies ran while one was open for 0% -> 0% of each run, Pallas kernels for 0% -> 0%
where the time goes in v1:
time: 150 us
  Pallas kernels  149 us (99%)
  local copies, waits for them, and re-layouts  1.54 us (1%)
    pallas_call x1, Pallas kernels, per_device(): pl.pallas_call(kernel, out_shape=jax.ShapeDtypeStruct((FEAT // 2, GROUP),...  149 us

profile of v1, /device:TPU:1, one launch (start us, length us, event | category | flops | bytes accessed | tf_op | source)
XLA Modules:
  0.0 150.1 jit_solution(12676705036662166608)
XLA Ops:
  0.0 148.6 %shard_map.73 = bf16[192,256]{1,0:T(8,128)(2,1)} custom-call(bf16[192,256]{1,0:T(8,128)(2,1)} %bitcast.9, bf16[192]{0:T(256)(128)(2,1)} %gain_ref.1, s32[2,256]{1,0:T(2,128)} %bitcast.10, f32[2,256]{1,0:T(2,128)} %bitcast.11, bf16[1,352,6144]{2,1,0:T(8,128)(2,1)} %bitcast.7, bf16[1,352,6144]{2,1,0:T(8,128)(2,1)} %bitcast.8, bf16[1,352,6144]{2,1,0:T(8,128)(2,1)} %wd_hbm.1), custom_call_target="tpu_custom_call" | custom-call | flops 13287555072 | bytes 12976128 | tf_op jit(solution)/shard_map/pallas_call | solution.py:499
  148.6 1.5 %copy.9 = bf16[256,192]{0,1:T(8,128)(2,1)} copy(bf16[256,192]{0,1:T(8,128)(2,1)} %bitcast.6) | data formatting | bytes 196608

commit v2 on v1

--- a/solution.py
+++ b/solution.py
@@ -272,16 +272,16 @@
                 scaled[:, at : at + 128] = (slab * gain[j : j + 1, :]).astype(BF16)
         sq[...] = squares
         acc[...] += lax.dot_general(
-            scaled[...], wgu[zi], (((1,), (1,)), ((), ())), preferred_element_type=F32
+            wgu[zi], scaled[...], (((1,), (1,)), ((), ())), preferred_element_type=F32
         )
 
         @pl.when(i == NZ - 1)
         def _():
-            total = jnp.sum(sq[...], axis=1, keepdims=True)
+            total = jnp.sum(jnp.transpose(sq[...]), axis=0, keepdims=True)
             scale = lax.rsqrt(total / D + NORM_EPS)
-            gate = acc[:, 0:HID] * scale
-            lift = acc[:, HID:] * scale
-            value = (gate / (1.0 + jnp.exp(-gate)) * lift).astype(BF16)
+            gate = acc[0:HID, :] * scale
+            lift = acc[HID:, :] * scale
+            value = jnp.transpose(gate / (1.0 + jnp.exp(-gate)) * lift).astype(BF16)
             for h in range(2):
                 hid[q, lax.rem(c + h, 2)] = value[h * ROWS : (h + 1) * ROWS]
             acc[...] = jnp.zeros_like(acc)
@@ -468,7 +468,7 @@
         pltpu.VMEM((blocks, HID, FEAT), BF16),
         pltpu.VMEM((CHUNKS, blocks, 2, ROWS, FEAT), BF16),
         pltpu.VMEM((2 * ROWS, NY * FEAT), BF16),
-        pltpu.VMEM((2 * ROWS, 2 * HID), F32),
+        pltpu.VMEM((2 * HID, 2 * ROWS), F32),
         pltpu.VMEM((2 * ROWS, 128), F32),
         pltpu.VMEM((CHUNKS, 2, ROWS, HID), BF16),
         pltpu.VMEM((NY, NZ, 16, 128), BF16),

time: 150 us -> 150 us (level)
  no operation moved by 1% of the time
where the time goes in v2:
time: 150 us
  Pallas kernels  149 us (99%)
  local copies, waits for them, and re-layouts  1.54 us (1%)
    pallas_call x1, Pallas kernels, per_device(): pl.pallas_call(kernel, out_shape=jax.ShapeDtypeStruct((FEAT // 2, GROUP),...  149 us

profile of v2, /device:TPU:1, one launch (start us, length us, event | category | flops | bytes accessed | tf_op | source)
XLA Modules:
  0.0 150.1 jit_solution(4013302426560651833)
XLA Ops:
  0.0 148.6 %shard_map.73 = bf16[192,256]{1,0:T(8,128)(2,1)} custom-call(bf16[192,256]{1,0:T(8,128)(2,1)} %bitcast.9, bf16[192]{0:T(256)(128)(2,1)} %gain_ref.1, s32[2,256]{1,0:T(2,128)} %bitcast.10, f32[2,256]{1,0:T(2,128)} %bitcast.11, bf16[1,352,6144]{2,1,0:T(8,128)(2,1)} %bitcast.7, bf16[1,352,6144]{2,1,0:T(8,128)(2,1)} %bitcast.8, bf16[1,352,6144]{2,1,0:T(8,128)(2,1)} %wd_hbm.1), custom_call_target="tpu_custom_call" | custom-call | flops 13287555072 | bytes 12976128 | tf_op jit(solution)/shard_map/pallas_call | solution.py:499
  148.6 1.5 %copy.9 = bf16[256,192]{0,1:T(8,128)(2,1)} copy(bf16[256,192]{0,1:T(8,128)(2,1)} %bitcast.6) | data formatting | bytes 196608

commit v3 on v2

--- a/solution.py
+++ b/solution.py
@@ -21,6 +21,7 @@
 STEPS = CHUNKS * NZ
 SECOND, THIRD, MULTIPLY = 2, 4, 5
 FARTHEST, NEIGHBOURS, FINISH = 1, 3, 5
+DRAIN_GATHER, DRAIN_REDUCE, COMBINE = 8, 7, 2
 LAG = NZ + MULTIPLY
 F32 = jnp.float32
 BF16 = jnp.bfloat16
@@ -36,7 +37,7 @@
     tok_hbm, gain_ref, ids_hbm, rw_hbm, wg_hbm, wu_hbm, wd_hbm,
     out_ref,
     wgu, wd, x, scaled, acc, sq, hid, gains,
-    ids_ref, rw_ref, tokx, sibtok, stage, mine, given, srecv, halves, fulls, zrecv, ret, part, partr,
+    ids_ref, rw_ref, tokx, sibtok, stage, mine, given, srecv, halves, fulls, zrecv, ret, comb, part, partr,
     wsem, dsem, tok_s, tok_r, disp_s, disp_r, gz_s, gz_r, gy_s, gy_r, gf_s, gf_r,
     z_s, z_r, y_s, y_r, f_s, f_r, b_s, b_r,
     sib_s, sib_r, h_s, h_r, w_s, w_r, zz_s, zz_r, ret_s, ret_r, part_s, part_r,
@@ -374,18 +375,72 @@
                     for k in range(max(1, chunk * PER), (chunk + 1) * PER):
                         retc(k).start()
 
+    def drain_gather(s):
+        q, i, zi = at_step(s)
+        for way in range(2):
+            yc(s, way).wait_send()
+            fc(s, way).wait_send()
+        for r in range(NY):
+            bc(s, r).wait_send()
+
+        @pl.when(i > 0)
+        def _():
+            zc(q, i).wait_send()
+
+    def drain_reduce(s):
+        q, i = out_step(s)
+        for way in range(2):
+            hc(s, way).wait_send()
+            wc(s, way).wait_send()
+        for r in range(NY):
+            sc(s, r).wait_send()
+
+        @pl.when(i > 0)
+        def _():
+            zzc(s).wait_send()
+
+    def combine(chunk):
+        for k in range(max(1, chunk * PER), (chunk + 1) * PER):
+            retc(k).wait_recv()
+        came = ret[chunk * PER : (chunk + 1) * PER].reshape(ROWS, FEAT)
+        spots = place[chunk * ROWS : (chunk + 1) * ROWS]
+        total = comb[...]
+        for k, dest in enumerate((dest0, dest1)):
+            pick = (spots == dest).astype(F32).astype(BF16)
+            total += rw_ref[k : k + 1, :] * lax.dot_general(
+                came, pick, (((0,), (0,)), ((), ())), preferred_element_type=F32
+            )
+        return total
+
     def step(t, carry):
         u = t - LAG
         stages = (
             (first, t, 0), (second, t, SECOND), (third, t, THIRD),
             (finish, u, FINISH), (neighbours, u, NEIGHBOURS), (farthest, u, FARTHEST),
-            (gate_up, t, MULTIPLY), (produce, u, 0),
         )
-        for stage_of, now, behind in stages:
-
-            @pl.when((now >= behind) & (now < STEPS + behind))
+
+        def run(stages):
+            for stage_of, now, behind in stages:
+
+                @pl.when((now >= behind) & (now < STEPS + behind))
+                def _():
+                    stage_of(now - behind)
+
+        run(stages)
+
+        @pl.when(t == MULTIPLY)
+        def _():
+            for load in loads + dloads:
+                load.wait()
+
+        run(((gate_up, t, MULTIPLY), (produce, u, 0)))
+        run(((drain_gather, t, DRAIN_GATHER), (drain_reduce, u, DRAIN_REDUCE)))
+
+        for chunk in range(CHUNKS - 1):
+
+            @pl.when(u == chunk * NZ + NZ - 1 + FINISH + COMBINE)
             def _():
-                stage_of(now - behind)
+                comb[...] = combine(chunk)
 
         return carry
 
@@ -395,22 +450,11 @@
         load.start()
     acc[...] = jnp.zeros_like(acc)
     sq[...] = jnp.zeros_like(sq)
-    for load in loads + dloads:
-        load.wait()
+    comb[...] = jnp.zeros_like(comb)
+    small[2].wait()
     lax.fori_loop(1, LAG + STEPS + FINISH, step, 0)
 
-    small[2].wait()
-    combined = jnp.zeros((FEAT, GROUP), F32)
-    for chunk in range(CHUNKS):
-        for k in range(max(1, chunk * PER), (chunk + 1) * PER):
-            retc(k).wait_recv()
-        came = ret[chunk * PER : (chunk + 1) * PER].reshape(ROWS, FEAT)
-        spots = place[chunk * ROWS : (chunk + 1) * ROWS]
-        for k, dest in enumerate((dest0, dest1)):
-            pick = (spots == dest).astype(F32).astype(BF16)
-            combined += rw_ref[k : k + 1, :] * lax.dot_general(
-                came, pick, (((0,), (0,)), ((), ())), preferred_element_type=F32
-            )
+    combined = combine(CHUNKS - 1)
     left = combined[:share]
     right = combined[share:]
     part[...] = jnp.where(c == 0, right, left)
@@ -432,30 +476,8 @@
         gyc(i, 1).wait_send()
         gfc(i).wait_send()
 
-    def drain(s, carry):
-        for way in range(2):
-            yc(s, way).wait_send()
-            fc(s, way).wait_send()
-            hc(s, way).wait_send()
-            wc(s, way).wait_send()
-        for r in range(NY):
-            bc(s, r).wait_send()
-            sc(s, r).wait_send()
-        q, i, zi = at_step(s)
-
-        @pl.when(i > 0)
-        def _():
-            zc(q, i).wait_send()
-
-        q, i = out_step(s)
-
-        @pl.when(i > 0)
-        def _():
-            zzc(s).wait_send()
-
-        return carry
-
-    lax.fori_loop(0, STEPS, drain, 0)
+    for s in range(STEPS + FINISH - DRAIN_REDUCE, STEPS):
+        drain_reduce(jnp.int32(s))
 
 
 def per_device(tokens, norm_gain, expert_ids, route_weights, gate_weight, up_weight, down_weight):
@@ -484,6 +506,7 @@
         pltpu.VMEM((STEPS, 2, ROWS, FEAT), BF16),
         pltpu.VMEM((CHUNKS, NZ, ROWS, FEAT), BF16),
         pltpu.VMEM((len(ROUTES), HALF, FEAT), BF16),
+        pltpu.VMEM((FEAT, GROUP), F32),
         pltpu.VMEM((FEAT // 2, GROUP), F32),
         pltpu.VMEM((FEAT // 2, GROUP), F32),
         dma((3 + 2 * blocks,)), dma((blocks,)),

time: 150 us -> 151 us (level)
  no operation moved by 1% of the time
where the time goes in v3:
time: 151 us; the launch traced here: 150 us
  Pallas kernels  149 us (99%)
  local copies, waits for them, and re-layouts  1.54 us (1%)
    pallas_call x1, Pallas kernels, per_device(): pl.pallas_call(kernel, out_shape=jax.ShapeDtypeStruct((FEAT // 2, GROUP),...  149 us

profile of v3, /device:TPU:1, one launch (start us, length us, event | category | flops | bytes accessed | tf_op | source)
XLA Modules:
  0.0 150.4 jit_solution(4259858758846830982)
XLA Ops:
  0.0 148.8 %shard_map.73 = bf16[192,256]{1,0:T(8,128)(2,1)} custom-call(bf16[192,256]{1,0:T(8,128)(2,1)} %bitcast.9, bf16[192]{0:T(256)(128)(2,1)} %gain_ref.1, s32[2,256]{1,0:T(2,128)} %bitcast.10, f32[2,256]{1,0:T(2,128)} %bitcast.11, bf16[1,352,6144]{2,1,0:T(8,128)(2,1)} %bitcast.7, bf16[1,352,6144]{2,1,0:T(8,128)(2,1)} %bitcast.8, bf16[1,352,6144]{2,1,0:T(8,128)(2,1)} %wd_hbm.1), custom_call_target="tpu_custom_call" | custom-call | flops 13287555072 | bytes 12976128 | tf_op jit(solution)/shard_map/pallas_call | solution.py:522
  148.8 1.5 %copy.9 = bf16[256,192]{0,1:T(8,128)(2,1)} copy(bf16[256,192]{0,1:T(8,128)(2,1)} %bitcast.6) | data formatting | bytes 196608

commit v4 on v3

--- a/solution.py
+++ b/solution.py
@@ -18,10 +18,12 @@
 PER = 2
 CHUNKS = len(ROUTES) // PER
 ROWS = PER * HALF
+FAR = tuple(k for k in range(len(ROUTES)) if ROUTES[k][1] == 1)
+HANDED = 1
 STEPS = CHUNKS * NZ
 SECOND, THIRD, MULTIPLY = 2, 4, 5
 FARTHEST, NEIGHBOURS, FINISH = 1, 3, 5
-DRAIN_GATHER, DRAIN_REDUCE, COMBINE = 8, 7, 2
+DRAIN_GATHER, DRAIN_REDUCE, COMBINE = 8, 7, 3
 LAG = NZ + MULTIPLY
 F32 = jnp.float32
 BF16 = jnp.bfloat16
@@ -37,9 +39,10 @@
     tok_hbm, gain_ref, ids_hbm, rw_hbm, wg_hbm, wu_hbm, wd_hbm,
     out_ref,
     wgu, wd, x, scaled, acc, sq, hid, gains,
-    ids_ref, rw_ref, tokx, sibtok, stage, mine, given, srecv, halves, fulls, zrecv, ret, comb, part, partr,
+    ids_ref, rw_ref, tokx, sibtok, stage, relay, back, farin, mine, given, srecv, halves, fulls, zrecv, ret, comb, part, partr,
     wsem, dsem, tok_s, tok_r, disp_s, disp_r, gz_s, gz_r, gy_s, gy_r, gf_s, gf_r,
     z_s, z_r, y_s, y_r, f_s, f_r, b_s, b_r,
+    fz_s, fz_r, fr_s, fr_r, rel_s, rel_r, back_s, back_r,
     sib_s, sib_r, h_s, h_r, w_s, w_r, zz_s, zz_r, ret_s, ret_r, part_s, part_r,
 ):
     xi = lax.axis_index("expert")
@@ -70,13 +73,23 @@
         dx, dd = ROUTES[k]
         return {"expert": lax.rem(xi + NX - dx, NX), "dp": lax.rem(di + dd, ND)}
 
+    def leg(dx, forward):
+        spot = lax.rem(di * NZ + z + (2 + 4 * c if forward else 6 - 4 * c), ND * NZ)
+        return {
+            "expert": lax.rem(xi + dx + NX, NX),
+            "tensor": tid(y, lax.rem(spot, NZ), c),
+            "dp": lax.div(spot, NZ),
+        }
+
     def rcopy(src, dst, ssem, rsem, dev):
         return pltpu.make_async_remote_copy(
             src_ref=src, dst_ref=dst, send_sem=ssem, recv_sem=rsem, device_id=dev, device_id_type=MESH
         )
 
     barrier = pltpu.get_barrier_semaphore()
-    partners = [sib, up, down] + [zdev(i) for i in range(1, NZ)] + [expert_of(k) for k in range(1, len(ROUTES))]
+    partners = [sib, up, down] + [zdev(i) for i in range(1, NZ)]
+    partners += [expert_of(k) for k in range(1, len(ROUTES)) if k not in FAR]
+    partners += [leg(dx, forward) for dx in range(NX) for forward in (True, False)]
     for dev in partners:
         pl.semaphore_signal(barrier, inc=1, device_id=dev, device_id_type=MESH)
 
@@ -147,12 +160,26 @@
     x[0, own, c, 0:HALF, :] = rows[0:HALF]
 
     def disp_copy(k):
-        target = x.at[k // PER, own, c, pl.ds((k % PER) * HALF, HALF)]
-        return rcopy(stage.at[k], target, disp_s.at[k], disp_r.at[k], expert_of(k))
+        q, span = k // PER, pl.ds((k % PER) * HALF, HALF)
+        if k in FAR:
+            target = x.at[q, y * NZ + lax.rem(z + 2, NZ), c, span]
+            return rcopy(relay.at[k - FAR[0]], target, disp_s.at[k], disp_r.at[k], leg(ROUTES[k][0], True))
+        return rcopy(stage.at[k], x.at[q, own, c, span], disp_s.at[k], disp_r.at[k], expert_of(k))
+
+    def relay_copy(part):
+        first_k = FAR[0] + part * PER
+        target = relay.at[pl.ds(part * PER, PER)]
+        return rcopy(stage.at[pl.ds(first_k, PER)], target, rel_s.at[part], rel_r.at[part], leg(0, True))
+
+    def relay_on(part):
+        relay_copy(part).wait_recv()
+        for k in range(FAR[0] + part * PER, FAR[0] + (part + 1) * PER):
+            disp_copy(k).start()
 
     for k in range(1, len(ROUTES)):
         stage[k] = rows[k * HALF : (k + 1) * HALF]
-        disp_copy(k).start()
+        if k < PER:
+            disp_copy(k).start()
 
     gain_row = jnp.concatenate(
         [first_core[share : share + 1, 0:share], second_core[share : share + 1, 0:share]], axis=1
@@ -196,6 +223,10 @@
         ref = x.at[q, b, c, pl.ds(way * (ROWS // 2), ROWS // 2)]
         return rcopy(ref, ref, f_s.at[s, way], f_r.at[s, way], (up, down)[way])
 
+    def fzc(q):
+        ref = x.at[q, lax.rem(y + 2, NY) * NZ + z, c]
+        return rcopy(ref, ref, fz_s.at[q], fz_r.at[q], zdev(HANDED))
+
     def bc(s, r):
         q, i, zi = at_step(s)
         b = lax.rem(y + r, NY) * NZ + zi
@@ -236,9 +267,17 @@
     def second(s):
         q, i, zi = at_step(s)
         yc(s, 0).wait_recv()
-        fc(s, 0).start()
+
+        @pl.when(i != HANDED)
+        def _():
+            fc(s, 0).start()
+
         yc(s, 1).wait_recv()
-        fc(s, 1).start()
+
+        @pl.when(i != HANDED)
+        def _():
+            fc(s, 1).start()
+
         bc(s, 3).start()
         bc(s, 1).start()
 
@@ -250,8 +289,19 @@
 
     def third(s):
         q, i, zi = at_step(s)
-        fc(s, 0).wait_recv()
-        fc(s, 1).wait_recv()
+        @pl.when(i != HANDED)
+        def _():
+            fc(s, 0).wait_recv()
+            fc(s, 1).wait_recv()
+
+        @pl.when(i == 0)
+        def _():
+            fzc(q).start()
+
+        @pl.when(i == HANDED)
+        def _():
+            fzc(q).wait_recv()
+
         bc(s, 2).start()
 
         @pl.when(s < NZ)
@@ -305,9 +355,25 @@
         q, i = out_step(s)
         return rcopy(mine.at[s, 0], zrecv.at[q, i], zz_s.at[q, i], zz_r.at[q, i], zdev(i))
 
+    def frc(s):
+        q, i = out_step(s)
+        return rcopy(mine.at[s, 2], farin.at[q], fr_s.at[q], fr_r.at[q], zdev(HANDED))
+
     def retc(k):
-        source = mine.at[k // PER * NZ + NZ - 1, 0, pl.ds((k % PER) * HALF, HALF)]
-        return rcopy(source, ret.at[k], ret_s.at[k], ret_r.at[k], group_of(k))
+        chunk, span = k // PER, pl.ds((k % PER) * HALF, HALF)
+        if k in FAR:
+            source = back.at[chunk - FAR[0] // PER, span]
+            return rcopy(source, ret.at[k], ret_s.at[k], ret_r.at[k], leg(-ROUTES[k][0], True))
+        return rcopy(mine.at[chunk * NZ + NZ - 1, 0, span], ret.at[k], ret_s.at[k], ret_r.at[k], group_of(k))
+
+    def back_copy(part):
+        chunk = FAR[0] // PER + part
+        return rcopy(mine.at[chunk * NZ + NZ - 1, 0], back.at[part], back_s.at[part], back_r.at[part], leg(0, True))
+
+    def back_on(part):
+        back_copy(part).wait_recv()
+        for k in range(FAR[0] + part * PER, FAR[0] + (part + 1) * PER):
+            retc(k).start()
 
     def produce(s):
         q, i = out_step(s)
@@ -325,22 +391,46 @@
         return mine[s, r].astype(F32) + srecv[s, r].astype(F32)
 
     def farthest(s):
-        mine[s, 2] = chip_sum(s, 2).astype(BF16)
-        hc(s, 0).start()
-        hc(s, 1).start()
+        q, i = out_step(s)
+        total = chip_sum(s, 2)
+
+        @pl.when(i == HANDED)
+        def _():
+            mine[s, 2] = total.astype(BF16)
+            frc(s).start()
+
+        @pl.when(i == 0)
+        def _():
+            frc(s - 1).wait_recv()
+            mine[s, 2] = (total + farin[q].astype(F32)).astype(BF16)
+
+        @pl.when(i > HANDED)
+        def _():
+            mine[s, 2] = total.astype(BF16)
+
+        @pl.when(i != HANDED)
+        def _():
+            hc(s, 0).start()
+            hc(s, 1).start()
 
     def neighbours(s):
+        q, i = out_step(s)
         half = ROWS // 2
-        total = chip_sum(s, 1)
-        hc(s, 0).wait_recv()
-        total = jnp.concatenate([total[:half] + halves[s, 0].astype(F32), total[half:]], axis=0)
-        mine[s, 1] = total.astype(BF16)
-        wc(s, 0).start()
-        total = chip_sum(s, 3)
-        hc(s, 1).wait_recv()
-        total = jnp.concatenate([total[:half], total[half:] + halves[s, 1].astype(F32)], axis=0)
-        mine[s, 3] = total.astype(BF16)
-        wc(s, 1).start()
+        for way, r in enumerate((1, 3)):
+            total = chip_sum(s, r)
+
+            @pl.when(i == HANDED)
+            def _():
+                mine[s, r] = total.astype(BF16)
+
+            @pl.when(i != HANDED)
+            def _():
+                hc(s, way).wait_recv()
+                parts = [total[:half], total[half:]]
+                parts[way] = parts[way] + halves[s, way].astype(F32)
+                mine[s, r] = jnp.concatenate(parts, axis=0).astype(BF16)
+
+            wc(s, way).start()
 
     def finish(s):
         q, i = out_step(s)
@@ -372,16 +462,27 @@
 
                 @pl.when(q == chunk)
                 def _():
-                    for k in range(max(1, chunk * PER), (chunk + 1) * PER):
-                        retc(k).start()
+                    if chunk * PER in FAR:
+                        back_copy(chunk - FAR[0] // PER).start()
+                    else:
+                        for k in range(max(1, chunk * PER), (chunk + 1) * PER):
+                            retc(k).start()
 
     def drain_gather(s):
         q, i, zi = at_step(s)
         for way in range(2):
             yc(s, way).wait_send()
-            fc(s, way).wait_send()
         for r in range(NY):
             bc(s, r).wait_send()
+
+        @pl.when(i != HANDED)
+        def _():
+            fc(s, 0).wait_send()
+            fc(s, 1).wait_send()
+
+        @pl.when(i == 0)
+        def _():
+            fzc(q).wait_send()
 
         @pl.when(i > 0)
         def _():
@@ -390,10 +491,18 @@
     def drain_reduce(s):
         q, i = out_step(s)
         for way in range(2):
-            hc(s, way).wait_send()
             wc(s, way).wait_send()
         for r in range(NY):
             sc(s, r).wait_send()
+
+        @pl.when(i != HANDED)
+        def _():
+            hc(s, 0).wait_send()
+            hc(s, 1).wait_send()
+
+        @pl.when(i == HANDED)
+        def _():
+            frc(s).wait_send()
 
         @pl.when(i > 0)
         def _():
@@ -428,6 +537,26 @@
 
         run(stages)
 
+        @pl.when(t == 1)
+        def _():
+            relay_copy(1).start()
+
+        @pl.when(t == 2)
+        def _():
+            relay_on(0)
+
+        @pl.when(t == 4)
+        def _():
+            relay_on(1)
+            for k in range((CHUNKS - 1) * PER, CHUNKS * PER):
+                disp_copy(k).start()
+
+        for part in range(len(FAR) // PER):
+
+            @pl.when(u == (FAR[0] // PER + part) * NZ + NZ + FINISH)
+            def _():
+                back_on(part)
+
         @pl.when(t == MULTIPLY)
         def _():
             for load in loads + dloads:
@@ -446,6 +575,7 @@
 
     open_chunk(0)
     first(jnp.int32(0))
+    relay_copy(0).start()
     for load in loads + dloads:
         load.start()
     acc[...] = jnp.zeros_like(acc)
@@ -469,6 +599,9 @@
     for k in range(1, len(ROUTES)):
         disp_copy(k).wait_send()
         retc(k).wait_send()
+    for part in range(len(FAR) // PER):
+        relay_copy(part).wait_send()
+        back_copy(part).wait_send()
     for i in range(NZ):
         if i > 0:
             gzc(i).wait_send()
@@ -499,6 +632,9 @@
         pltpu.VMEM((FEAT // 2 + 16, GROUP), BF16),
         pltpu.VMEM((FEAT // 2 + 16, GROUP), BF16),
         pltpu.VMEM((len(ROUTES), HALF, FEAT), BF16),
+        pltpu.VMEM((len(FAR), HALF, FEAT), BF16),
+        pltpu.VMEM((len(FAR) // PER, ROWS, FEAT), BF16),
+        pltpu.VMEM((CHUNKS, ROWS, FEAT), BF16),
         pltpu.VMEM((STEPS, NY, ROWS, FEAT), BF16),
         pltpu.VMEM((STEPS, NY, ROWS, FEAT), BF16),
         pltpu.VMEM((STEPS, NY, ROWS, FEAT), BF16),
@@ -514,6 +650,8 @@
         dma((NZ,)), dma((NZ,)), dma((NZ, 2)), dma((NZ, 2)), dma((NZ,)), dma((NZ,)),
         dma((CHUNKS, NZ)), dma((CHUNKS, NZ)), dma((STEPS, 2)), dma((STEPS, 2)),
         dma((STEPS, 2)), dma((STEPS, 2)), dma((STEPS, NY)), dma((STEPS, NY)),
+        dma((CHUNKS,)), dma((CHUNKS,)), dma((CHUNKS,)), dma((CHUNKS,)),
+        dma((len(FAR) // PER,)), dma((len(FAR) // PER,)), dma((len(FAR) // PER,)), dma((len(FAR) // PER,)),
         dma((STEPS, NY)), dma((STEPS, NY)), dma((STEPS, 2)), dma((STEPS, 2)),
         dma((STEPS, 2)), dma((STEPS, 2)), dma((CHUNKS, NZ)), dma((CHUNKS, NZ)),
         dma((len(ROUTES),)), dma((len(ROUTES),)), dma, dma,

time: 151 us -> 152 us (level)
  no operation moved by 1% of the time
where the time goes in v4:
time: 152 us; the launch traced here: 151 us
  Pallas kernels  150 us (99%)
  local copies, waits for them, and re-layouts  1.54 us (1%)
    pallas_call x1, Pallas kernels, per_device(): pl.pallas_call(kernel, out_shape=jax.ShapeDtypeStruct((FEAT // 2, GROUP),...  150 us

profile of v4, /device:TPU:1, one launch (start us, length us, event | category | flops | bytes accessed | tf_op | source)
XLA Modules:
  0.0 151.4 jit_solution(4915395993055754300)
XLA Ops:
  0.0 149.9 %shard_map.73 = bf16[192,256]{1,0:T(8,128)(2,1)} custom-call(bf16[192,256]{1,0:T(8,128)(2,1)} %bitcast.9, bf16[192]{0:T(256)(128)(2,1)} %gain_ref.1, s32[2,256]{1,0:T(2,128)} %bitcast.10, f32[2,256]{1,0:T(2,128)} %bitcast.11, bf16[1,352,6144]{2,1,0:T(8,128)(2,1)} %bitcast.7, bf16[1,352,6144]{2,1,0:T(8,128)(2,1)} %bitcast.8, bf16[1,352,6144]{2,1,0:T(8,128)(2,1)} %wd_hbm.1), custom_call_target="tpu_custom_call" | custom-call | flops 13287555072 | bytes 12976128 | tf_op jit(solution)/shard_map/pallas_call | solution.py:660
  149.9 1.5 %copy.9 = bf16[256,192]{0,1:T(8,128)(2,1)} copy(bf16[256,192]{0,1:T(8,128)(2,1)} %bitcast.6) | data formatting | bytes 196608

commit v5 on v4

--- a/solution.py
+++ b/solution.py
@@ -22,8 +22,8 @@
 HANDED = 1
 STEPS = CHUNKS * NZ
 SECOND, THIRD, MULTIPLY = 2, 4, 5
-FARTHEST, NEIGHBOURS, FINISH = 1, 3, 5
-DRAIN_GATHER, DRAIN_REDUCE, COMBINE = 8, 7, 3
+NEIGHBOURS, FINISH = 2, 4
+DRAIN_GATHER, DRAIN_REDUCE, COMBINE = 8, 6, 3
 LAG = NZ + MULTIPLY
 F32 = jnp.float32
 BF16 = jnp.bfloat16
@@ -38,12 +38,12 @@
 def kernel(
     tok_hbm, gain_ref, ids_hbm, rw_hbm, wg_hbm, wu_hbm, wd_hbm,
     out_ref,
-    wgu, wd, x, scaled, acc, sq, hid, gains,
-    ids_ref, rw_ref, tokx, sibtok, stage, relay, back, farin, mine, given, srecv, halves, fulls, zrecv, ret, comb, part, partr,
+    wgu, wd, wd2, x, scaled, acc, sq, hid, hidout, hidin, gains,
+    ids_ref, rw_ref, tokx, sibtok, stage, relay, back, farin, mine, halves, fulls, zrecv, ret, comb, part, partr,
     wsem, dsem, tok_s, tok_r, disp_s, disp_r, gz_s, gz_r, gy_s, gy_r, gf_s, gf_r,
     z_s, z_r, y_s, y_r, f_s, f_r, b_s, b_r,
     fz_s, fz_r, fr_s, fr_r, rel_s, rel_r, back_s, back_r,
-    sib_s, sib_r, h_s, h_r, w_s, w_r, zz_s, zz_r, ret_s, ret_r, part_s, part_r,
+    wd2_s, wd2_r, hid_s, hid_r, h_s, h_r, w_s, w_r, zz_s, zz_r, ret_s, ret_r, part_s, part_r,
 ):
     xi = lax.axis_index("expert")
     di = lax.axis_index("dp")
@@ -147,6 +147,10 @@
         pltpu.make_async_copy(wd_hbm.at[0, :, pl.ds(j * FEAT, FEAT)], wd.at[j], dsem.at[j])
         for j in range(NY * NZ)
     ]
+    shared = [
+        rcopy(wd_hbm.at[0, :, pl.ds(j * FEAT, FEAT)], wd2.at[j], wd2_s.at[j], wd2_r.at[j], sib)
+        for j in range(NY * NZ)
+    ]
 
     tok_copy.wait_recv()
     here = tokx[...].astype(F32)
@@ -307,6 +311,9 @@
         @pl.when(s < NZ)
         def _():
             gfc(i).wait_recv()
+
+    def hidc(q):
+        return rcopy(hidout.at[q], hidin.at[q], hid_s.at[q], hid_r.at[q], sib)
 
     def gate_up(s):
         q, i, zi = at_step(s)
@@ -332,17 +339,16 @@
             scale = lax.rsqrt(total / D + NORM_EPS)
             gate = acc[0:HID, :] * scale
             lift = acc[HID:, :] * scale
-            value = jnp.transpose(gate / (1.0 + jnp.exp(-gate)) * lift).astype(BF16)
-            for h in range(2):
-                hid[q, lax.rem(c + h, 2)] = value[h * ROWS : (h + 1) * ROWS]
+            value = jnp.transpose(gate / (1.0 + jnp.exp(-gate)) * lift)
+            lower, upper = value[:ROWS], value[ROWS:]
+            hidout[q] = jnp.where(c == 0, upper, lower).astype(BF16)
+            hidc(q).start()
+            hid[q] = jnp.where(c == 0, lower, upper).astype(BF16)
             acc[...] = jnp.zeros_like(acc)
             sq[...] = jnp.zeros_like(sq)
 
     def out_step(s):
         return lax.div(s, NZ), (NZ - 1) - lax.rem(s, NZ)
-
-    def sc(s, r):
-        return rcopy(given.at[s, r], srecv.at[s, r], sib_s.at[s, r], sib_r.at[s, r], sib)
 
     def hc(s, way):
         span = pl.ds(way * (ROWS // 2), ROWS // 2)
@@ -378,63 +384,54 @@
     def produce(s):
         q, i = out_step(s)
         zi = xor4(z, i)
-        left = hid[q].reshape(2 * ROWS, HID)
+
+        @pl.when(i == NZ - 1)
+        def _():
+            hidc(q).wait_recv()
+
         for r in (2, 1, 3, 0):
             b = lax.rem(y + r, NY) * NZ + zi
-            block = jnp.dot(left, wd[b], preferred_element_type=F32).astype(BF16)
-            given[s, r] = block[ROWS:]
-            sc(s, r).start()
-            mine[s, r] = block[:ROWS]
-
-    def chip_sum(s, r):
-        sc(s, r).wait_recv()
-        return mine[s, r].astype(F32) + srecv[s, r].astype(F32)
-
-    def farthest(s):
-        q, i = out_step(s)
-        total = chip_sum(s, 2)
-
-        @pl.when(i == HANDED)
-        def _():
-            mine[s, 2] = total.astype(BF16)
-            frc(s).start()
-
-        @pl.when(i == 0)
-        def _():
-            frc(s - 1).wait_recv()
-            mine[s, 2] = (total + farin[q].astype(F32)).astype(BF16)
-
-        @pl.when(i > HANDED)
-        def _():
-            mine[s, 2] = total.astype(BF16)
-
-        @pl.when(i != HANDED)
-        def _():
-            hc(s, 0).start()
-            hc(s, 1).start()
+            total = jnp.dot(hid[q], wd[b], preferred_element_type=F32)
+            total += jnp.dot(hidin[q], wd2[b], preferred_element_type=F32)
+            if r != 2:
+                mine[s, r] = total.astype(BF16)
+                continue
+
+            @pl.when(i == HANDED)
+            def _():
+                mine[s, r] = total.astype(BF16)
+                frc(s).start()
+
+            @pl.when(i == 0)
+            def _():
+                frc(s - 1).wait_recv()
+                mine[s, r] = (total + farin[q].astype(F32)).astype(BF16)
+
+            @pl.when(i > HANDED)
+            def _():
+                mine[s, r] = total.astype(BF16)
+
+            @pl.when(i != HANDED)
+            def _():
+                hc(s, 0).start()
+                hc(s, 1).start()
 
     def neighbours(s):
         q, i = out_step(s)
         half = ROWS // 2
         for way, r in enumerate((1, 3)):
-            total = chip_sum(s, r)
-
-            @pl.when(i == HANDED)
-            def _():
-                mine[s, r] = total.astype(BF16)
 
             @pl.when(i != HANDED)
             def _():
                 hc(s, way).wait_recv()
-                parts = [total[:half], total[half:]]
-                parts[way] = parts[way] + halves[s, way].astype(F32)
-                mine[s, r] = jnp.concatenate(parts, axis=0).astype(BF16)
+                span = pl.ds(way * half, half)
+                mine[s, r, span] = (mine[s, r, span].astype(F32) + halves[s, way].astype(F32)).astype(BF16)
 
             wc(s, way).start()
 
     def finish(s):
         q, i = out_step(s)
-        total = chip_sum(s, 0)
+        total = mine[s, 0].astype(F32)
         wc(s, 0).wait_recv()
         total = total + fulls[s, 0].astype(F32)
         wc(s, 1).wait_recv()
@@ -492,9 +489,6 @@
         q, i = out_step(s)
         for way in range(2):
             wc(s, way).wait_send()
-        for r in range(NY):
-            sc(s, r).wait_send()
-
         @pl.when(i != HANDED)
         def _():
             hc(s, 0).wait_send()
@@ -525,7 +519,7 @@
         u = t - LAG
         stages = (
             (first, t, 0), (second, t, SECOND), (third, t, THIRD),
-            (finish, u, FINISH), (neighbours, u, NEIGHBOURS), (farthest, u, FARTHEST),
+            (finish, u, FINISH), (neighbours, u, NEIGHBOURS),
         )
 
         def run(stages):
@@ -559,10 +553,17 @@
 
         @pl.when(t == MULTIPLY)
         def _():
-            for load in loads + dloads:
+            for load in loads:
                 load.wait()
 
-        run(((gate_up, t, MULTIPLY), (produce, u, 0)))
+        @pl.when(u == 0)
+        def _():
+            for load in dloads:
+                load.wait()
+            for copy in shared:
+                copy.wait_recv()
+
+        run(((produce, u, 0), (gate_up, t, MULTIPLY)))
         run(((drain_gather, t, DRAIN_GATHER), (drain_reduce, u, DRAIN_REDUCE)))
 
         for chunk in range(CHUNKS - 1):
@@ -576,7 +577,7 @@
     open_chunk(0)
     first(jnp.int32(0))
     relay_copy(0).start()
-    for load in loads + dloads:
+    for load in loads + dloads + shared:
         load.start()
     acc[...] = jnp.zeros_like(acc)
     sq[...] = jnp.zeros_like(sq)
@@ -596,6 +597,10 @@
 
     part_copy.wait_send()
     tok_copy.wait_send()
+    for copy in shared:
+        copy.wait_send()
+    for q in range(CHUNKS):
+        hidc(q).wait_send()
     for k in range(1, len(ROUTES)):
         disp_copy(k).wait_send()
         retc(k).wait_send()
@@ -621,11 +626,14 @@
     scratch = [
         pltpu.VMEM((NZ, 2 * HID, NY * FEAT), BF16),
         pltpu.VMEM((blocks, HID, FEAT), BF16),
+        pltpu.VMEM((blocks, HID, FEAT), BF16),
         pltpu.VMEM((CHUNKS, blocks, 2, ROWS, FEAT), BF16),
         pltpu.VMEM((2 * ROWS, NY * FEAT), BF16),
         pltpu.VMEM((2 * HID, 2 * ROWS), F32),
         pltpu.VMEM((2 * ROWS, 128), F32),
-        pltpu.VMEM((CHUNKS, 2, ROWS, HID), BF16),
+        pltpu.VMEM((CHUNKS, ROWS, HID), BF16),
+        pltpu.VMEM((CHUNKS, ROWS, HID), BF16),
+        pltpu.VMEM((CHUNKS, ROWS, HID), BF16),
         pltpu.VMEM((NY, NZ, 16, 128), BF16),
         pltpu.VMEM((2, GROUP), jnp.int32),
         pltpu.VMEM((2, GROUP), F32),
@@ -635,8 +643,6 @@
         pltpu.VMEM((len(FAR), HALF, FEAT), BF16),
         pltpu.VMEM((len(FAR) // PER, ROWS, FEAT), BF16),
         pltpu.VMEM((CHUNKS, ROWS, FEAT), BF16),
-        pltpu.VMEM((STEPS, NY, ROWS, FEAT), BF16),
-        pltpu.VMEM((STEPS, NY, ROWS, FEAT), BF16),
         pltpu.VMEM((STEPS, NY, ROWS, FEAT), BF16),
         pltpu.VMEM((STEPS, 2, ROWS // 2, FEAT), BF16),
         pltpu.VMEM((STEPS, 2, ROWS, FEAT), BF16),
@@ -652,7 +658,7 @@
         dma((STEPS, 2)), dma((STEPS, 2)), dma((STEPS, NY)), dma((STEPS, NY)),
         dma((CHUNKS,)), dma((CHUNKS,)), dma((CHUNKS,)), dma((CHUNKS,)),
         dma((len(FAR) // PER,)), dma((len(FAR) // PER,)), dma((len(FAR) // PER,)), dma((len(FAR) // PER,)),
-        dma((STEPS, NY)), dma((STEPS, NY)), dma((STEPS, 2)), dma((STEPS, 2)),
+        dma((blocks,)), dma((blocks,)), dma((CHUNKS,)), dma((CHUNKS,)), dma((STEPS, 2)), dma((STEPS, 2)),
         dma((STEPS, 2)), dma((STEPS, 2)), dma((CHUNKS, NZ)), dma((CHUNKS, NZ)),
         dma((len(ROUTES),)), dma((len(ROUTES),)), dma, dma,
     ]

time: 152 us -> 152 us (level); the launches traced: 151 us -> 149 us
  Pallas kernels: 150 us -> 148 us
    pallas_call x1, Pallas kernels: 150 us -> 148 us  [per_device(): pl.pallas_call(kernel, out_shape=jax.ShapeDtypeStruct((FEAT // 2, GROUP),...]
where the time goes in v5:
time: 152 us; the launch traced here: 149 us
  Pallas kernels  148 us (97%)
  local copies, waits for them, and re-layouts  1.54 us (1%)
    pallas_call x1, Pallas kernels, per_device(): pl.pallas_call(kernel, out_shape=jax.ShapeDtypeStruct((FEAT // 2, GROUP),...  148 us

profile of v5, /device:TPU:1, one launch (start us, length us, event | category | flops | bytes accessed | tf_op | source)
XLA Modules:
  0.0 149.2 jit_solution(10271037228819141713)
XLA Ops:
  0.0 147.7 %shard_map.73 = bf16[192,256]{1,0:T(8,128)(2,1)} custom-call(bf16[192,256]{1,0:T(8,128)(2,1)} %bitcast.9, bf16[192]{0:T(256)(128)(2,1)} %gain_ref.1, s32[2,256]{1,0:T(2,128)} %bitcast.10, f32[2,256]{1,0:T(2,128)} %bitcast.11, bf16[1,352,6144]{2,1,0:T(8,128)(2,1)} %bitcast.7, bf16[1,352,6144]{2,1,0:T(8,128)(2,1)} %bitcast.8, bf16[1,352,6144]{2,1,0:T(8,128)(2,1)} %wd_hbm.1), custom_call_target="tpu_custom_call" | custom-call | flops 13287555072 | bytes 12976128 | tf_op jit(solution)/shard_map/pallas_call | solution.py:666
  147.7 1.5 %copy.9 = bf16[256,192]{0,1:T(8,128)(2,1)} copy(bf16[256,192]{0,1:T(8,128)(2,1)} %bitcast.6) | data formatting | bytes 196608

commit v6 on v3

--- a/solution.py
+++ b/solution.py
@@ -21,7 +21,6 @@
 STEPS = CHUNKS * NZ
 SECOND, THIRD, MULTIPLY = 2, 4, 5
 FARTHEST, NEIGHBOURS, FINISH = 1, 3, 5
-DRAIN_GATHER, DRAIN_REDUCE, COMBINE = 8, 7, 2
 LAG = NZ + MULTIPLY
 F32 = jnp.float32
 BF16 = jnp.bfloat16
@@ -37,7 +36,7 @@
     tok_hbm, gain_ref, ids_hbm, rw_hbm, wg_hbm, wu_hbm, wd_hbm,
     out_ref,
     wgu, wd, x, scaled, acc, sq, hid, gains,
-    ids_ref, rw_ref, tokx, sibtok, stage, mine, given, srecv, halves, fulls, zrecv, ret, comb, part, partr,
+    ids_ref, rw_ref, tokx, sibtok, stage, mine, given, srecv, halves, fulls, zrecv, ret, part, partr,
     wsem, dsem, tok_s, tok_r, disp_s, disp_r, gz_s, gz_r, gy_s, gy_r, gf_s, gf_r,
     z_s, z_r, y_s, y_r, f_s, f_r, b_s, b_r,
     sib_s, sib_r, h_s, h_r, w_s, w_r, zz_s, zz_r, ret_s, ret_r, part_s, part_r,
@@ -152,7 +151,8 @@
 
     for k in range(1, len(ROUTES)):
         stage[k] = rows[k * HALF : (k + 1) * HALF]
-        disp_copy(k).start()
+        if k < 2 * PER:
+            disp_copy(k).start()
 
     gain_row = jnp.concatenate(
         [first_core[share : share + 1, 0:share], second_core[share : share + 1, 0:share]], axis=1
@@ -399,25 +399,15 @@
         def _():
             zzc(s).wait_send()
 
-    def combine(chunk):
-        for k in range(max(1, chunk * PER), (chunk + 1) * PER):
-            retc(k).wait_recv()
-        came = ret[chunk * PER : (chunk + 1) * PER].reshape(ROWS, FEAT)
-        spots = place[chunk * ROWS : (chunk + 1) * ROWS]
-        total = comb[...]
-        for k, dest in enumerate((dest0, dest1)):
-            pick = (spots == dest).astype(F32).astype(BF16)
-            total += rw_ref[k : k + 1, :] * lax.dot_general(
-                came, pick, (((0,), (0,)), ((), ())), preferred_element_type=F32
-            )
-        return total
+    def drain(stage_of, steps):
+        def one(s, carry):
+            stage_of(s)
+            return carry
+
+        lax.fori_loop(0, steps, one, 0)
 
     def step(t, carry):
         u = t - LAG
-        stages = (
-            (first, t, 0), (second, t, SECOND), (third, t, THIRD),
-            (finish, u, FINISH), (neighbours, u, NEIGHBOURS), (farthest, u, FARTHEST),
-        )
 
         def run(stages):
             for stage_of, now, behind in stages:
@@ -426,21 +416,37 @@
                 def _():
                     stage_of(now - behind)
 
-        run(stages)
+        run((
+            (first, t, 0), (second, t, SECOND), (third, t, THIRD),
+            (finish, u, FINISH), (neighbours, u, NEIGHBOURS), (farthest, u, FARTHEST),
+        ))
+
+        for chunk in range(2, CHUNKS):
+
+            @pl.when(t == 2 * chunk - 1)
+            def _():
+                for k in range(chunk * PER, (chunk + 1) * PER):
+                    disp_copy(k).start()
 
         @pl.when(t == MULTIPLY)
         def _():
-            for load in loads + dloads:
+            for load in loads:
                 load.wait()
 
+        @pl.when(u == 0)
+        def _():
+            for load in dloads:
+                load.wait()
+
         run(((gate_up, t, MULTIPLY), (produce, u, 0)))
-        run(((drain_gather, t, DRAIN_GATHER), (drain_reduce, u, DRAIN_REDUCE)))
-
-        for chunk in range(CHUNKS - 1):
-
-            @pl.when(u == chunk * NZ + NZ - 1 + FINISH + COMBINE)
-            def _():
-                comb[...] = combine(chunk)
+
+        @pl.when(u == STEPS)
+        def _():
+            drain(drain_gather, STEPS)
+
+        @pl.when(u == STEPS + 1)
+        def _():
+            drain(drain_reduce, STEPS - NZ)
 
         return carry
 
@@ -450,11 +456,20 @@
         load.start()
     acc[...] = jnp.zeros_like(acc)
     sq[...] = jnp.zeros_like(sq)
-    comb[...] = jnp.zeros_like(comb)
+    lax.fori_loop(1, LAG + STEPS + FINISH, step, 0)
+
     small[2].wait()
-    lax.fori_loop(1, LAG + STEPS + FINISH, step, 0)
-
-    combined = combine(CHUNKS - 1)
+    combined = jnp.zeros((FEAT, GROUP), F32)
+    for chunk in range(CHUNKS):
+        for k in range(max(1, chunk * PER), (chunk + 1) * PER):
+            retc(k).wait_recv()
+        came = ret[chunk * PER : (chunk + 1) * PER].reshape(ROWS, FEAT)
+        spots = place[chunk * ROWS : (chunk + 1) * ROWS]
+        for k, dest in enumerate((dest0, dest1)):
+            pick = (spots == dest).astype(F32).astype(BF16)
+            combined += rw_ref[k : k + 1, :] * lax.dot_general(
+                came, pick, (((0,), (0,)), ((), ())), preferred_element_type=F32
+            )
     left = combined[:share]
     right = combined[share:]
     part[...] = jnp.where(c == 0, right, left)
@@ -476,7 +491,7 @@
         gyc(i, 1).wait_send()
         gfc(i).wait_send()
 
-    for s in range(STEPS + FINISH - DRAIN_REDUCE, STEPS):
+    for s in range(STEPS - NZ, STEPS):
         drain_reduce(jnp.int32(s))
 
 
@@ -506,7 +521,6 @@
         pltpu.VMEM((STEPS, 2, ROWS, FEAT), BF16),
         pltpu.VMEM((CHUNKS, NZ, ROWS, FEAT), BF16),
         pltpu.VMEM((len(ROUTES), HALF, FEAT), BF16),
-        pltpu.VMEM((FEAT, GROUP), F32),
         pltpu.VMEM((FEAT // 2, GROUP), F32),
         pltpu.VMEM((FEAT // 2, GROUP), F32),
         dma((3 + 2 * blocks,)), dma((blocks,)),

time: 151 us -> 148 us (0.980)
  Pallas kernels: 149 us -> 146 us
    pallas_call x1, Pallas kernels: 149 us -> 146 us  [per_device(): pl.pallas_call(kernel, out_shape=jax.ShapeDtypeStruct((FEAT // 2, GROUP),...]
where the time goes in v6:
time: 148 us
  Pallas kernels  146 us (99%)
  local copies, waits for them, and re-layouts  1.54 us (1%)
    pallas_call x1, Pallas kernels, per_device(): pl.pallas_call(kernel, out_shape=jax.ShapeDtypeStruct((FEAT // 2, GROUP),...  146 us

profile of v6, /device:TPU:1, one launch (start us, length us, event | category | flops | bytes accessed | tf_op | source)
XLA Modules:
  0.0 147.7 jit_solution(4535177230262327198)
XLA Ops:
  0.0 146.2 %shard_map.73 = bf16[192,256]{1,0:T(8,128)(2,1)} custom-call(bf16[192,256]{1,0:T(8,128)(2,1)} %bitcast.9, bf16[192]{0:T(256)(128)(2,1)} %gain_ref.1, s32[2,256]{1,0:T(2,128)} %bitcast.10, f32[2,256]{1,0:T(2,128)} %bitcast.11, bf16[1,352,6144]{2,1,0:T(8,128)(2,1)} %bitcast.7, bf16[1,352,6144]{2,1,0:T(8,128)(2,1)} %bitcast.8, bf16[1,352,6144]{2,1,0:T(8,128)(2,1)} %wd_hbm.1), custom_call_target="tpu_custom_call" | custom-call | flops 13287555072 | bytes 12976128 | tf_op jit(solution)/shard_map/pallas_call | solution.py:536
  146.2 1.5 %copy.9 = bf16[256,192]{0,1:T(8,128)(2,1)} copy(bf16[256,192]{0,1:T(8,128)(2,1)} %bitcast.6) | data formatting | bytes 196608

commit v7 on v6

--- a/solution.py
+++ b/solution.py
@@ -19,6 +19,7 @@
 CHUNKS = len(ROUTES) // PER
 ROWS = PER * HALF
 STEPS = CHUNKS * NZ
+GIVER, HANDED = 2, 3
 SECOND, THIRD, MULTIPLY = 2, 4, 5
 FARTHEST, NEIGHBOURS, FINISH = 1, 3, 5
 LAG = NZ + MULTIPLY
@@ -36,9 +37,10 @@
     tok_hbm, gain_ref, ids_hbm, rw_hbm, wg_hbm, wu_hbm, wd_hbm,
     out_ref,
     wgu, wd, x, scaled, acc, sq, hid, gains,
-    ids_ref, rw_ref, tokx, sibtok, stage, mine, given, srecv, halves, fulls, zrecv, ret, part, partr,
+    ids_ref, rw_ref, tokx, sibtok, stage, farin, mine, given, srecv, halves, fulls, zrecv, ret, part, partr,
     wsem, dsem, tok_s, tok_r, disp_s, disp_r, gz_s, gz_r, gy_s, gy_r, gf_s, gf_r,
     z_s, z_r, y_s, y_r, f_s, f_r, b_s, b_r,
+    fz_s, fz_r, fr_s, fr_r,
     sib_s, sib_r, h_s, h_r, w_s, w_r, zz_s, zz_r, ret_s, ret_r, part_s, part_r,
 ):
     xi = lax.axis_index("expert")
@@ -196,6 +198,10 @@
         ref = x.at[q, b, c, pl.ds(way * (ROWS // 2), ROWS // 2)]
         return rcopy(ref, ref, f_s.at[s, way], f_r.at[s, way], (up, down)[way])
 
+    def fzc(q):
+        ref = x.at[q, lax.rem(y + 2, NY) * NZ + xor4(z, GIVER), c]
+        return rcopy(ref, ref, fz_s.at[q], fz_r.at[q], zdev(1))
+
     def bc(s, r):
         q, i, zi = at_step(s)
         b = lax.rem(y + r, NY) * NZ + zi
@@ -236,9 +242,17 @@
     def second(s):
         q, i, zi = at_step(s)
         yc(s, 0).wait_recv()
-        fc(s, 0).start()
+
+        @pl.when(i != HANDED)
+        def _():
+            fc(s, 0).start()
+
         yc(s, 1).wait_recv()
-        fc(s, 1).start()
+
+        @pl.when(i != HANDED)
+        def _():
+            fc(s, 1).start()
+
         bc(s, 3).start()
         bc(s, 1).start()
 
@@ -250,8 +264,19 @@
 
     def third(s):
         q, i, zi = at_step(s)
-        fc(s, 0).wait_recv()
-        fc(s, 1).wait_recv()
+        @pl.when(i != HANDED)
+        def _():
+            fc(s, 0).wait_recv()
+            fc(s, 1).wait_recv()
+
+        @pl.when(i == GIVER)
+        def _():
+            fzc(q).start()
+
+        @pl.when(i == HANDED)
+        def _():
+            fzc(q).wait_recv()
+
         bc(s, 2).start()
 
         @pl.when(s < NZ)
@@ -305,6 +330,10 @@
         q, i = out_step(s)
         return rcopy(mine.at[s, 0], zrecv.at[q, i], zz_s.at[q, i], zz_r.at[q, i], zdev(i))
 
+    def frc(s):
+        q, i = out_step(s)
+        return rcopy(mine.at[s, 2], farin.at[q], fr_s.at[q], fr_r.at[q], zdev(1))
+
     def retc(k):
         source = mine.at[k // PER * NZ + NZ - 1, 0, pl.ds((k % PER) * HALF, HALF)]
         return rcopy(source, ret.at[k], ret_s.at[k], ret_r.at[k], group_of(k))
@@ -325,22 +354,46 @@
         return mine[s, r].astype(F32) + srecv[s, r].astype(F32)
 
     def farthest(s):
-        mine[s, 2] = chip_sum(s, 2).astype(BF16)
-        hc(s, 0).start()
-        hc(s, 1).start()
+        q, i = out_step(s)
+        total = chip_sum(s, 2)
+
+        @pl.when(i == HANDED)
+        def _():
+            mine[s, 2] = total.astype(BF16)
+            frc(s).start()
+
+        @pl.when(i == GIVER)
+        def _():
+            frc(s - 1).wait_recv()
+            mine[s, 2] = (total + farin[q].astype(F32)).astype(BF16)
+
+        @pl.when((i != HANDED) & (i != GIVER))
+        def _():
+            mine[s, 2] = total.astype(BF16)
+
+        @pl.when(i != HANDED)
+        def _():
+            hc(s, 0).start()
+            hc(s, 1).start()
 
     def neighbours(s):
+        q, i = out_step(s)
         half = ROWS // 2
-        total = chip_sum(s, 1)
-        hc(s, 0).wait_recv()
-        total = jnp.concatenate([total[:half] + halves[s, 0].astype(F32), total[half:]], axis=0)
-        mine[s, 1] = total.astype(BF16)
-        wc(s, 0).start()
-        total = chip_sum(s, 3)
-        hc(s, 1).wait_recv()
-        total = jnp.concatenate([total[:half], total[half:] + halves[s, 1].astype(F32)], axis=0)
-        mine[s, 3] = total.astype(BF16)
-        wc(s, 1).start()
+        for way, r in enumerate((1, 3)):
+            total = chip_sum(s, r)
+
+            @pl.when(i == HANDED)
+            def _():
+                mine[s, r] = total.astype(BF16)
+
+            @pl.when(i != HANDED)
+            def _():
+                hc(s, way).wait_recv()
+                parts = [total[:half], total[half:]]
+                parts[way] = parts[way] + halves[s, way].astype(F32)
+                mine[s, r] = jnp.concatenate(parts, axis=0).astype(BF16)
+
+            wc(s, way).start()
 
     def finish(s):
         q, i = out_step(s)
@@ -379,9 +432,17 @@
         q, i, zi = at_step(s)
         for way in range(2):
             yc(s, way).wait_send()
-            fc(s, way).wait_send()
         for r in range(NY):
             bc(s, r).wait_send()
+
+        @pl.when(i != HANDED)
+        def _():
+            fc(s, 0).wait_send()
+            fc(s, 1).wait_send()
+
+        @pl.when(i == GIVER)
+        def _():
+            fzc(q).wait_send()
 
         @pl.when(i > 0)
         def _():
@@ -390,10 +451,18 @@
     def drain_reduce(s):
         q, i = out_step(s)
         for way in range(2):
-            hc(s, way).wait_send()
             wc(s, way).wait_send()
         for r in range(NY):
             sc(s, r).wait_send()
+
+        @pl.when(i != HANDED)
+        def _():
+            hc(s, 0).wait_send()
+            hc(s, 1).wait_send()
+
+        @pl.when(i == HANDED)
+        def _():
+            frc(s).wait_send()
 
         @pl.when(i > 0)
         def _():
@@ -514,6 +583,7 @@
         pltpu.VMEM((FEAT // 2 + 16, GROUP), BF16),
         pltpu.VMEM((FEAT // 2 + 16, GROUP), BF16),
         pltpu.VMEM((len(ROUTES), HALF, FEAT), BF16),
+        pltpu.VMEM((CHUNKS, ROWS, FEAT), BF16),
         pltpu.VMEM((STEPS, NY, ROWS, FEAT), BF16),
         pltpu.VMEM((STEPS, NY, ROWS, FEAT), BF16),
         pltpu.VMEM((STEPS, NY, ROWS, FEAT), BF16),
@@ -528,6 +598,7 @@
         dma((NZ,)), dma((NZ,)), dma((NZ, 2)), dma((NZ, 2)), dma((NZ,)), dma((NZ,)),
         dma((CHUNKS, NZ)), dma((CHUNKS, NZ)), dma((STEPS, 2)), dma((STEPS, 2)),
         dma((STEPS, 2)), dma((STEPS, 2)), dma((STEPS, NY)), dma((STEPS, NY)),
+        dma((CHUNKS,)), dma((CHUNKS,)), dma((CHUNKS,)), dma((CHUNKS,)),
         dma((STEPS, NY)), dma((STEPS, NY)), dma((STEPS, 2)), dma((STEPS, 2)),
         dma((STEPS, 2)), dma((STEPS, 2)), dma((CHUNKS, NZ)), dma((CHUNKS, NZ)),
         dma((len(ROUTES),)), dma((len(ROUTES),)), dma, dma,

time: 148 us -> 148 us (level)
  no operation moved by 1% of the time
where the time goes in v7:
time: 148 us
  Pallas kernels  146 us (99%)
  local copies, waits for them, and re-layouts  1.54 us (1%)
    pallas_call x1, Pallas kernels, per_device(): pl.pallas_call(kernel, out_shape=jax.ShapeDtypeStruct((FEAT // 2, GROUP),...  146 us

profile of v7, /device:TPU:1, one launch (start us, length us, event | category | flops | bytes accessed | tf_op | source)
XLA Modules:
  0.0 147.5 jit_solution(12717200557631917526)
XLA Ops:
  0.0 146.0 %shard_map.73 = bf16[192,256]{1,0:T(8,128)(2,1)} custom-call(bf16[192,256]{1,0:T(8,128)(2,1)} %bitcast.9, bf16[192]{0:T(256)(128)(2,1)} %gain_ref.1, s32[2,256]{1,0:T(2,128)} %bitcast.10, f32[2,256]{1,0:T(2,128)} %bitcast.11, bf16[1,352,6144]{2,1,0:T(8,128)(2,1)} %bitcast.7, bf16[1,352,6144]{2,1,0:T(8,128)(2,1)} %bitcast.8, bf16[1,352,6144]{2,1,0:T(8,128)(2,1)} %wd_hbm.1), custom_call_target="tpu_custom_call" | custom-call | flops 13287555072 | bytes 12976128 | tf_op jit(solution)/shard_map/pallas_call | solution.py:607
  146.0 1.5 %copy.9 = bf16[256,192]{0,1:T(8,128)(2,1)} copy(bf16[256,192]{0,1:T(8,128)(2,1)} %bitcast.6) | data formatting | bytes 196608

commit v8 on v7

--- a/solution.py
+++ b/solution.py
@@ -20,8 +20,8 @@
 ROWS = PER * HALF
 STEPS = CHUNKS * NZ
 GIVER, HANDED = 2, 3
-SECOND, THIRD, MULTIPLY = 2, 4, 5
-FARTHEST, NEIGHBOURS, FINISH = 1, 3, 5
+SECOND, THIRD, MULTIPLY = 3, 6, 7
+FARTHEST, NEIGHBOURS, FINISH = 1, 4, 7
 LAG = NZ + MULTIPLY
 F32 = jnp.float32
 BF16 = jnp.bfloat16
@@ -513,7 +513,7 @@
         def _():
             drain(drain_gather, STEPS)
 
-        @pl.when(u == STEPS + 1)
+        @pl.when(u == STEPS + FINISH - 3)
         def _():
             drain(drain_reduce, STEPS - NZ)
 

time: 148 us -> 153 us (1.034)
  Pallas kernels: 146 us -> 152 us
    pallas_call x1, Pallas kernels: 146 us -> 152 us  [per_device(): pl.pallas_call(kernel, out_shape=jax.ShapeDtypeStruct((FEAT // 2, GROUP),...]
where the time goes in v8:
time: 153 us
  Pallas kernels  152 us (99%)
  local copies, waits for them, and re-layouts  1.54 us (1%)
    pallas_call x1, Pallas kernels, per_device(): pl.pallas_call(kernel, out_shape=jax.ShapeDtypeStruct((FEAT // 2, GROUP),...  152 us

profile of v8, /device:TPU:1, one launch (start us, length us, event | category | flops | bytes accessed | tf_op | source)
XLA Modules:
  0.0 153.3 jit_solution(2036155052980025947)
XLA Ops:
  0.0 151.7 %shard_map.73 = bf16[192,256]{1,0:T(8,128)(2,1)} custom-call(bf16[192,256]{1,0:T(8,128)(2,1)} %bitcast.9, bf16[192]{0:T(256)(128)(2,1)} %gain_ref.1, s32[2,256]{1,0:T(2,128)} %bitcast.10, f32[2,256]{1,0:T(2,128)} %bitcast.11, bf16[1,352,6144]{2,1,0:T(8,128)(2,1)} %bitcast.7, bf16[1,352,6144]{2,1,0:T(8,128)(2,1)} %bitcast.8, bf16[1,352,6144]{2,1,0:T(8,128)(2,1)} %wd_hbm.1), custom_call_target="tpu_custom_call" | custom-call | flops 13287555072 | bytes 12976128 | tf_op jit(solution)/shard_map/pallas_call | solution.py:607
  151.7 1.5 %copy.9 = bf16[256,192]{0,1:T(8,128)(2,1)} copy(bf16[256,192]{0,1:T(8,128)(2,1)} %bitcast.6) | data formatting | bytes 196608
